TPU v7x, 256 devices: a whole 4x4x8 slice. The times are simulated.
256 devices in a mesh: dp: 16 (over z, y_hi), expert: 16 (over y_lo, x, core).
Axes of the slice: x: 4, y: 4 (y_hi: 2, y_lo: 2; y = y_hi * 2 + y_lo), z: 8, core: 2. Of those that a mesh axis runs over, the one named last changes fastest.
Arguments:
- tokens: bfloat16 [65536, 1024], P(('dp', 'expert')), may hold values from -6 to 6
- token_picks: int32 [256, 16, 32], P(('dp', 'expert')), may hold values from 0 to 255, as said below
- gate_values: float32 [256, 16, 32], P(('dp', 'expert')), may hold values from 0.05 to 1
- w_in: bfloat16 [16, 1024, 2048], P('expert'), may hold values from -0.1875 to 0.1875
- w_out: bfloat16 [16, 2048, 1024], P('expert'), may hold values from -0.125 to 0.125
- cotangent: bfloat16 [65536, 1024], P(('dp', 'expert')), may hold values from -24 to 24
Outputs:
- mixed: bfloat16 [65536, 1024], P(('dp', 'expert'))
- token_grad: bfloat16 [65536, 1024], P(('dp', 'expert'))
- grad_in: bfloat16 [1024, 16, 2048], P('dp', 'expert')
- grad_out: bfloat16 [1024, 16, 2048], P('dp', 'expert')
Inputs may be any that keep to these rules, and one draw needn't show every extreme that they name: `token_picks`: entry (i, e, p) is one of device i's 256 local token rows that expert e takes; for each device and expert the 32 rows are distinct.
All inputs are finite; a program needn't handle non-finite values.
Results may differ from a plain program's by a relative error of at most 0.024.
Values may be sent and summed in bfloat16 or wider, within the bound.
A program may use at most 128 MiB of HBM per device.

v0:
```python
import jax
import jax.numpy as jnp
from jax import lax
from jax.sharding import PartitionSpec as P


def gelu_exact(values):
    return jax.nn.gelu(values, approximate=False)


def on_device(tokens, token_picks, gate_values, w_in, w_out, cotangent):
    local_tokens = tokens.shape[0]
    width = tokens.shape[1]
    experts = token_picks.shape[1]
    per_pick = token_picks.shape[2]
    local_experts = w_in.shape[0]
    owners = lax.axis_size("expert")
    flat_index = token_picks[0].reshape(-1)
    gate_flat = gate_values[0].reshape(-1)
    selector = (flat_index[:, None] == jnp.arange(local_tokens, dtype=jnp.int32)[None, :]).astype(
        jnp.bfloat16
    )
    send_tokens = jnp.take(tokens, flat_index, axis=0).reshape(experts, per_pick, width)
    received = lax.all_to_all(send_tokens, "expert", split_axis=0, concat_axis=0, tiled=True)
    grouped = received.reshape(owners, local_experts, per_pick, width)
    pre_act = jnp.einsum("sepd,edh->seph", grouped, w_in, preferred_element_type=jnp.float32)
    activated = gelu_exact(pre_act).astype(jnp.bfloat16)
    expert_out = jnp.einsum(
        "seph,ehd->sepd", activated, w_out, preferred_element_type=jnp.float32
    ).astype(jnp.bfloat16)
    returned = lax.all_to_all(
        expert_out.reshape(experts, per_pick, width),
        "expert",
        split_axis=0,
        concat_axis=0,
        tiled=True,
    )
    weighted = returned.reshape(-1, width).astype(jnp.float32) * gate_flat[:, None]
    mixed = (
        jnp.zeros((local_tokens, width), jnp.float32)
        .at[flat_index]
        .add(weighted)
        .astype(jnp.bfloat16)
    )
    grad_sent = (
        jnp.take(cotangent, flat_index, axis=0).astype(jnp.float32) * gate_flat[:, None]
    ).astype(jnp.bfloat16)
    grad_sent = grad_sent.reshape(experts, per_pick, width)
    grad_received = lax.all_to_all(grad_sent, "expert", split_axis=0, concat_axis=0, tiled=True)
    grad_rows = grad_received.reshape(owners, local_experts, per_pick, width)
    act_f, gelu_back = jax.vjp(gelu_exact, pre_act)
    act_rows = act_f.astype(jnp.bfloat16)
    grad_act = jnp.einsum("sepd,ehd->seph", grad_rows, w_out, preferred_element_type=jnp.float32)
    grad_pre = gelu_back(grad_act)[0].astype(jnp.bfloat16)
    grad_taken = jnp.einsum(
        "seph,edh->sepd", grad_pre, w_in, preferred_element_type=jnp.float32
    ).astype(jnp.bfloat16)
    grad_back = lax.all_to_all(
        grad_taken.reshape(experts, per_pick, width),
        "expert",
        split_axis=0,
        concat_axis=0,
        tiled=True,
    )
    summed = lax.psum_scatter(
        jnp.concatenate(
            [
                jnp.einsum("sepd,seph->deh", grouped, grad_pre, preferred_element_type=jnp.float32),
                jnp.einsum(
                    "sepd,seph->deh", grad_rows, act_rows, preferred_element_type=jnp.float32
                ),
            ],
            axis=1,
        ).astype(jnp.bfloat16),
        "dp",
        scatter_dimension=0,
        tiled=True,
    )
    grad_in = summed[:, :local_experts, :]
    grad_out = summed[:, local_experts:, :]
    token_grad = jnp.einsum(
        "kt,kd->td", selector, grad_back.reshape(-1, width), preferred_element_type=jnp.float32
    ).astype(jnp.bfloat16)
    return (mixed, token_grad, grad_in, grad_out)


def solution(mesh):
    in_specs = (
        P(("dp", "expert"), None),
        P(("dp", "expert"), None, None),
        P(("dp", "expert"), None, None),
        P("expert", None, None),
        P("expert", None, None),
        P(("dp", "expert"), None),
    )
    out_specs = (
        P(("dp", "expert"), None),
        P(("dp", "expert"), None),
        P("dp", "expert", None),
        P("dp", "expert", None),
    )
    return jax.shard_map(
        on_device, mesh=mesh, in_specs=in_specs, out_specs=out_specs, check_vma=False
    )
```

profile of v0, /device:TPU:4, one launch (start us, length us, event | category | flops | bytes accessed | tf_op | source)
XLA Modules:
  0.0 516.1 jit_solution(15934920506194462674)
XLA Ops:
  8.6 2.0 gather_fusion
  11.8 5.8 %all-to-all-start = ((bf16[16,32,1024]{2,1,0:T(8,128)(2,1)}), bf16[16,32,1024]{2,1,0:T(8,128)(2,1)S(1)}, u32[]{:S(2)}, u32[]{:S(2)}) async-start(bf16[16,32,1024]{2,1,0:T(8,128)(2,1)} %bitcast.1), calls=%async_computation | async-start | bytes 2097152 | tf_op jit(solution)/shard_map/all_to_all | solution.py:24
  17.8 2.1 gather_fusion.1
  21.1 9.8 %all-to-all-done = bf16[16,32,1024]{2,1,0:T(8,128)(2,1)S(1)} async-done(((bf16[16,32,1024]{2,1,0:T(8,128)(2,1)}), bf16[16,32,1024]{2,1,0:T(8,128)(2,1)S(1)}, u32[]{:S(2)}, u32[]{:S(2)}) %all-to-all-start) | async-done | bytes 1048608 | tf_op jit(solution)/shard_map/all_to_all | solution.py:24
  31.0 7.4 %all-to-all-start.2 = ((bf16[16,32,1024]{2,1,0:T(8,128)(2,1)}), bf16[16,32,1024]{2,1,0:T(8,128)(2,1)}, u32[]{:S(2)}, u32[]{:S(2)}) async-start(bf16[16,32,1024]{2,1,0:T(8,128)(2,1)} %bitcast.18), calls=%async_computation.2 | async-start | bytes 2097152 | tf_op jit(solution)/shard_map/all_to_all | solution.py:49
  38.4 6.5 %fusion.16 = f32[16,32,2048]{2,1,0:T(8,128)} fusion(bf16[16,32,1024]{2,1,0:T(8,128)(2,1)S(1)} %all-to-all-done, bf16[1,1024,2048]{2,1,0:T(8,128)(2,1)} %param.11), kind=kOutput, calls=%fused_computation.30 | convolution fusion | flops 2147483648 | bytes 9437184 | tf_op jit(solution)/shard_map/sepd,edh->seph/dot_general | solution.py:26
  44.9 6.9 %all-to-all-done.2 = bf16[16,32,1024]{2,1,0:T(8,128)(2,1)} async-done(((bf16[16,32,1024]{2,1,0:T(8,128)(2,1)}), bf16[16,32,1024]{2,1,0:T(8,128)(2,1)}, u32[]{:S(2)}, u32[]{:S(2)}) %all-to-all-start.2) | async-done | bytes 1048608 | tf_op jit(solution)/shard_map/all_to_all | solution.py:49
  51.8 13.0 %fusion.27 = bf16[1024,1,2048]{0,2,1:T(8,128)(2,1)S(1)} fusion(bf16[16,32,1024]{2,1,0:T(8,128)(2,1)} %all-to-all-done.2, f32[16,32,2048]{2,1,0:T(8,128)} %fusion.16), kind=kOutput, calls=%fused_computation.42 | convolution fusion | flops 2217738240 | bytes 9437184 | tf_op jit(solution)/shard_map/sepd,seph->deh/dot_general | solution.py:69
  64.8 13.1 %fusion.30 = bf16[16,32,2048]{2,1,0:T(8,128)(2,1)S(1)} fusion(f32[16,32,2048]{2,1,0:T(8,128)S(1)} %copy-done.10, bf16[16,32,1024]{2,1,0:T(8,128)(2,1)} %all-to-all-done.2, bf16[1,2048,1024]{2,1,0:T(8,128)(2,1)S(1)} %copy-done.8), kind=kOutput, calls=%fused_computation.43 | convolution fusion | flops 2222981120 | bytes 11534336 | tf_op jit(solution)/shard_map/sepd,ehd->seph/dot_general | solution.py:53
  77.9 1.4 copy-done.11
  79.3 4.3 fusion.26
  83.6 6.2 %pad_maximum_fusion = bf16[1024,2,2048]{0,2,1:T(8,128)(2,1)} fusion(bf16[1024,1,2048]{0,2,1:T(8,128)(2,1)S(1)} %fusion.27, bf16[1024,1,2048]{0,2,1:T(8,128)(2,1)} %fusion.26), kind=kLoop, calls=%fused_computation.3 | loop fusion | flops 4194304 | bytes 16777216 | tf_op jit(solution)/shard_map/concatenate | solution.py:66
  89.8 21.5 %copy.14 = bf16[1024,2,2048]{2,1,0:T(2,128)(2,1)} copy(bf16[1024,2,2048]{0,2,1:T(8,128)(2,1)} %pad_maximum_fusion) | data formatting | bytes 16777216 | tf_op jit(solution)/shard_map/concatenate | solution.py:66
  111.3 14.6 %fusion.38 = bf16[16,32,1024]{2,1,0:T(8,128)(2,1)} fusion(bf16[1,2048,1024]{2,1,0:T(8,128)(2,1)} %param.12, f32[16,32,2048]{2,1,0:T(8,128)} %fusion.16), kind=kOutput, calls=%fused_computation.49 | convolution fusion | flops 2216165376 | bytes 9437184 | tf_op jit(solution)/shard_map/seph,ehd->sepd/dot_general | solution.py:28
  126.0 6.8 %all-to-all-start.1 = ((bf16[16,32,1024]{2,1,0:T(8,128)(2,1)}), bf16[16,32,1024]{2,1,0:T(8,128)(2,1)S(1)}, u32[]{:S(2)}, u32[]{:S(2)}) async-start(bf16[16,32,1024]{2,1,0:T(8,128)(2,1)} %fusion.38), calls=%async_computation.1 | async-start | bytes 2097152 | tf_op jit(solution)/shard_map/all_to_all | solution.py:31
  132.8 6.2 %fusion.35 = bf16[16,32,1024]{2,1,0:T(8,128)(2,1)} fusion(bf16[16,32,2048]{2,1,0:T(8,128)(2,1)} %copy-done.11, bf16[1,1024,2048]{2,1,0:T(8,128)(2,1)} %param.11), kind=kOutput, calls=%fused_computation.48 | convolution fusion | flops 2148007936 | bytes 7340032 | tf_op jit(solution)/shard_map/seph,edh->sepd/dot_general | solution.py:55
  139.0 13.1 %all-to-all-done.1 = bf16[16,32,1024]{2,1,0:T(8,128)(2,1)S(1)} async-done(((bf16[16,32,1024]{2,1,0:T(8,128)(2,1)}), bf16[16,32,1024]{2,1,0:T(8,128)(2,1)S(1)}, u32[]{:S(2)}, u32[]{:S(2)}) %all-to-all-start.1) | async-done | bytes 1048608 | tf_op jit(solution)/shard_map/all_to_all | solution.py:31
  152.1 5.1 all-to-all-start.3
  158.6 5.9 %scatter_custom_fusion = f32[256,1024]{1,0:T(8,128)} fusion(s32[512]{0:T(512)S(1)} %bitcast.153, bf16[512,1024]{1,0:T(8,128)(2,1)S(1)} %bitcast.151, f32[512]{0:T(512)S(1)} %copy-done.6, f32[]{:T(128)} %constant.0.clone.1), kind=kCustom, calls=%fused_computation.46 | custom fusion | flops 1572864 | bytes 2099204 | tf_op jit(solution)/shard_map/scatter-add | solution.py:42
  164.5 2.1 convert_element_type.43
  166.6 11.7 %all-to-all-done.3 = bf16[16,32,1024]{2,1,0:T(8,128)(2,1)S(1)} async-done(((bf16[16,32,1024]{2,1,0:T(8,128)(2,1)}), bf16[16,32,1024]{2,1,0:T(8,128)(2,1)S(1)}, u32[]{:S(2)}, u32[]{:S(2)}) %all-to-all-start.3) | async-done | bytes 1048608 | tf_op jit(solution)/shard_map/all_to_all | solution.py:58
  178.2 1.4 convolution_convert_fusion
  179.6 325.8 %all-reduce.3.cloned.1.call-done = bf16[1024,2,2048]{2,1,0:T(2,128)(2,1)} async-done(((bf16[1024,2,2048]{2,1,0:T(2,128)(2,1)}), bf16[1024,2,2048]{2,1,0:T(2,128)(2,1)}) %all-reduce.3.cloned.1.call-update) | async-done | bytes 8388624
  505.4 2.1 constant_dynamic-slice_fusion.1
  (37 shorter events, 6.4 us)
Async XLA Ops:
  7.2 1.4 copy-start
  8.0 0.6 copy-start.2
  10.7 7.0 %copy-start.7 = (f32[1,16,32]{2,1,0:T(8,128)S(1)}, f32[1,16,32]{2,1,0:T(8,128)}, u32[]{:S(2)}) copy-start(f32[1,16,32]{2,1,0:T(8,128)} %param.10) | copy-start | bytes 6148
  10.7 7.1 %copy-start.1 = (bf16[256,1024]{1,0:T(8,128)(2,1)S(1)}, bf16[256,1024]{1,0:T(8,128)(2,1)}, u32[]{:S(2)}) copy-start(bf16[256,1024]{1,0:T(8,128)(2,1)} %param.13) | copy-start | bytes 1572868
  11.8 19.1 %all-to-all-start = ((bf16[16,32,1024]{2,1,0:T(8,128)(2,1)}), bf16[16,32,1024]{2,1,0:T(8,128)(2,1)S(1)}, u32[]{:S(2)}, u32[]{:S(2)}) async-start(bf16[16,32,1024]{2,1,0:T(8,128)(2,1)} %bitcast.1), calls=%async_computation | async-start | bytes 2097152 | tf_op jit(solution)/shard_map/all_to_all | solution.py:24
  17.8 2.1 copy-start.5
  31.0 20.8 %all-to-all-start.2 = ((bf16[16,32,1024]{2,1,0:T(8,128)(2,1)}), bf16[16,32,1024]{2,1,0:T(8,128)(2,1)}, u32[]{:S(2)}, u32[]{:S(2)}) async-start(bf16[16,32,1024]{2,1,0:T(8,128)(2,1)} %bitcast.18), calls=%async_computation.2 | async-start | bytes 2097152 | tf_op jit(solution)/shard_map/all_to_all | solution.py:49
  38.3 467.1 %all-reduce.3.cloned.1.call-start = ((), (), s32[]{:S(2)}) async-start(), calls=%async_computation.4 | async-start | bytes 16777216
  51.8 13.0 %copy-start.8 = (bf16[1,2048,1024]{2,1,0:T(8,128)(2,1)S(1)}, bf16[1,2048,1024]{2,1,0:T(8,128)(2,1)}, u32[]{:S(2)}) copy-start(bf16[1,2048,1024]{2,1,0:T(8,128)(2,1)} %param.12) | copy-start | bytes 12582916
  51.8 13.0 %copy-start.10 = (f32[16,32,2048]{2,1,0:T(8,128)S(1)}, f32[16,32,2048]{2,1,0:T(8,128)}, u32[]{:S(2)}) copy-start(f32[16,32,2048]{2,1,0:T(8,128)} %fusion.16) | copy-start | bytes 12582916
  77.9 1.4 copy-start.11
  126.0 26.2 %all-to-all-start.1 = ((bf16[16,32,1024]{2,1,0:T(8,128)(2,1)}), bf16[16,32,1024]{2,1,0:T(8,128)(2,1)S(1)}, u32[]{:S(2)}, u32[]{:S(2)}) async-start(bf16[16,32,1024]{2,1,0:T(8,128)(2,1)} %fusion.38), calls=%async_computation.1 | async-start | bytes 2097152 | tf_op jit(solution)/shard_map/all_to_all | solution.py:31
  132.7 24.5 %copy-start.4 = (s32[1,16,32]{2,1,0:T(8,128)S(1)}, s32[1,16,32]{2,1,0:T(8,128)}, u32[]{:S(2)}) copy-start(s32[1,16,32]{2,1,0:T(8,128)} %param.9) | copy-start | bytes 6148
  132.8 24.6 %copy-start.9 = (u32[256]{0:T(256)S(1)}, u32[256]{0:T(256)}, u32[]{:S(2)}) copy-start(u32[256]{0:T(256)} %constant.83) | copy-start | bytes 3076
  132.8 25.8 %copy-start.6 = (f32[512]{0:T(512)S(1)}, f32[512]{0:T(512)}, u32[]{:S(2)}) copy-start(f32[512]{0:T(512)} %copy-done.5) | copy-start | bytes 6148
  139.0 39.2 %copy-start.3 = (s32[512]{0:T(512)S(1)}, s32[512]{0:T(512)}, u32[]{:S(2)}) copy-start(s32[512]{0:T(512)} %copy-done.2) | copy-start | bytes 6148
  152.1 26.1 %all-to-all-start.3 = ((bf16[16,32,1024]{2,1,0:T(8,128)(2,1)}), bf16[16,32,1024]{2,1,0:T(8,128)(2,1)S(1)}, u32[]{:S(2)}, u32[]{:S(2)}) async-start(bf16[16,32,1024]{2,1,0:T(8,128)(2,1)} %fusion.35), calls=%async_computation.3 | async-start | bytes 2097152 | tf_op jit(solution)/shard_map/all_to_all | solution.py:58
Sparse Core Ops, SparseCore 0:
  111.5 393.9 all-reduce.2
where the time goes:
time: 520 us; the launch traced here: 516 us
  waiting for transfers between devices  367 us (71%)
  matrix products  59.2 us (11%)
  local copies, waits for them, and re-layouts  32.9 us (6%)
  starting transfers between devices  25.1 us (5%)
  other arithmetic  16.7 us (3%)
  between operations  14.8 us (3%)
    unnamed x2, waiting for transfers between devices  326 us
    concatenate x1, local copies, waits for them, and re-layouts, on_device(): jnp.concatenate([jnp.einsum('sepd,seph->deh', grouped, grad_pre, preferre...  21.5 us
    dot_general x1, matrix products, on_device(): jnp.einsum('seph,ehd->sepd', activated, w_out, preferred_element_type=jnp...  14.6 us
    dot_general x1, matrix products, on_device(): jnp.einsum('sepd,ehd->seph', grad_rows, w_out, preferred_element_type=jnp...  13.1 us
    all_to_all x1, waiting for transfers between devices, on_device(): lax.all_to_all(expert_out.reshape(experts, per_pick, width), 'expert', sp...  13.1 us
    dot_general x1, matrix products, on_device(): jnp.einsum('sepd,seph->deh', grad_rows, act_rows, preferred_element_type=...  13 us
    all_to_all x1, waiting for transfers between devices, on_device(): lax.all_to_all(grad_taken.reshape(experts, per_pick, width), 'expert', sp...  11.7 us
  transfers between devices with their start and end apart: 5, of which 5 were waited for; matrix products, arithmetic and copies ran while one was open for 8% of the time, Pallas kernels for 0%

commit v1 on v0

v1 whole, which is shorter than its diff:
```python
import functools

import jax
import jax.numpy as jnp
from jax import lax
from jax.experimental import pallas as pl
from jax.experimental.pallas import tpu as pltpu
from jax.sharding import PartitionSpec as P

MESH = pl.DeviceIdType.MESH
BF = jnp.bfloat16
F32 = jnp.float32
NT = (((1,), (1,)), ((), ()))


def dot(a, b):
    return jnp.dot(a, b, preferred_element_type=F32)


def dot_nt(a, b):
    return lax.dot_general(a, b, NT, preferred_element_type=F32)


def kernel(
    n_dp, n_ex,
    tok, pick, gate, win_hbm, wout_hbm, cot,
    mixed, tgrad, gin, gout,
    win, wout, stok, sgrad, taken, gsent, act, dgel, gpre, eout, gtak, rout, rgrad,
    xt, part, ring, ysend, yrecv,
    wsem, dsend, drecv, rsend, rrecv, ysem_s, ysem_r,
):
    nz = n_dp // 2
    tokens, width = tok.shape
    per = pick.shape[2]
    rows = n_ex * per
    hidden = win.shape[1]
    blk = width // nz
    half_rows = blk // 2
    half = hidden // 2
    r = lax.axis_index("dp")
    me = lax.axis_index("expert")
    z = r // 2
    yh = r % 2
    up = (r + 2) % n_dp
    down = (r + n_dp - 2) % n_dp
    across = r + 1 - 2 * yh

    barrier = pltpu.get_barrier_semaphore()

    def greet(k, c):
        pl.semaphore_signal(
            barrier, inc=1, device_id={"expert": (me + k) % n_ex}, device_id_type=MESH
        )
        return c

    lax.fori_loop(1, n_ex, greet, 0)
    for other in (up, down, across):
        pl.semaphore_signal(barrier, inc=1, device_id={"dp": other}, device_id_type=MESH)

    load_in = pltpu.make_async_copy(win_hbm.at[0], win, wsem.at[0])
    load_out = pltpu.make_async_copy(wout_hbm.at[0], wout, wsem.at[1])
    load_in.start()
    load_out.start()

    p2 = pick[0].astype(F32).astype(BF)
    g = gate[0]
    g1 = g.astype(BF)
    g2 = (g - g1.astype(F32)).astype(BF)
    g3 = (g - g1.astype(F32) - g2.astype(F32)).astype(BF)
    row_e = lax.broadcasted_iota(jnp.int32, (rows, n_ex), 0) // per
    expert_of = (row_e == lax.broadcasted_iota(jnp.int32, (rows, n_ex), 1)).astype(F32).astype(BF)
    place = lax.broadcasted_iota(jnp.int32, (rows, per), 0) % per
    here = place == lax.broadcasted_iota(jnp.int32, (rows, per), 1)

    def column(values):
        return jnp.sum(jnp.where(here, values, 0.0), axis=1, keepdims=True)

    pick_col = column(dot(expert_of, p2))
    gate_col = column(dot(expert_of, g1) + dot(expert_of, g2) + dot(expert_of, g3))
    lanes = lax.broadcasted_iota(jnp.int32, (rows, tokens), 1).astype(F32)
    sel = (lanes == pick_col).astype(F32).astype(BF)
    spread = dot_nt(p2, here.astype(F32).astype(BF))
    own_e = lax.broadcasted_iota(jnp.int32, (n_ex, rows), 0) == (
        lax.broadcasted_iota(jnp.int32, (n_ex, rows), 1) // per
    )
    pick_row = jnp.sum(jnp.where(own_e, spread, 0.0), axis=0, keepdims=True)
    selt = lax.broadcasted_iota(jnp.int32, (tokens, rows), 0).astype(F32) == pick_row
    gspread = (
        dot_nt(g1, here.astype(F32).astype(BF))
        + dot_nt(g2, here.astype(F32).astype(BF))
        + dot_nt(g3, here.astype(F32).astype(BF))
    )
    gate_row = jnp.sum(jnp.where(own_e, gspread, 0.0), axis=0, keepdims=True)

    stok[...] = dot(sel, tok[...]).astype(BF)

    pl.semaphore_wait(barrier, n_ex + 2)

    def exchange(which, src, dst, peer):
        return pltpu.make_async_remote_copy(
            src_ref=src.at[pl.ds(peer * per, per)],
            dst_ref=dst.at[pl.ds(me * per, per)],
            send_sem=dsend.at[which, peer],
            recv_sem=drecv.at[which, me],
            device_id={"expert": peer},
            device_id_type=MESH,
        )

    def send_all(which, src, dst):
        def body(i, c):
            k = 1 + i // 2
            peer = (me + k * (1 - 2 * (i % 2)) + n_ex) % n_ex
            exchange(which, src, dst, peer).start()
            return c

        lax.fori_loop(0, n_ex - 1, body, 0)
        own = pl.ds(me * per, per)
        dst[own, :] = src[own, :]

    def recv_all(which, src, dst):
        def body(k, c):
            peer = (me + k) % n_ex
            pltpu.make_async_remote_copy(
                src_ref=src.at[pl.ds(peer * per, per)],
                dst_ref=dst.at[pl.ds(peer * per, per)],
                send_sem=dsend.at[which, peer],
                recv_sem=drecv.at[which, peer],
                device_id={"expert": peer},
                device_id_type=MESH,
            ).wait_recv()
            return c

        lax.fori_loop(1, n_ex, body, 0)

    def sent_all(which, src, dst):
        def body(k, c):
            exchange(which, src, dst, (me + k) % n_ex).wait_send()
            return c

        lax.fori_loop(1, n_ex, body, 0)

    send_all(0, stok, taken)
    sgrad[...] = (dot(sel, cot[...]) * gate_col).astype(BF)
    send_all(1, sgrad, gsent)

    load_in.wait()
    recv_all(0, stok, taken)

    tile = min(256, hidden)

    def forward(j, c):
        cols = pl.ds(pl.multiple_of(j * tile, tile), tile)
        pre = dot(taken[...], win[:, cols])
        cdf = 0.5 * (1.0 + lax.erf(pre * 0.7071067811865476))
        act[:, cols] = (pre * cdf).astype(BF)
        dgel[:, cols] = cdf + pre * (0.3989422804014327 * jnp.exp(-0.5 * pre * pre))
        return c

    lax.fori_loop(0, hidden // tile, forward, 0)
    xt[1] = taken[...].T

    load_out.wait()
    wtile = min(256, width)

    def out_proj(j, c):
        cols = pl.ds(pl.multiple_of(j * wtile, wtile), wtile)
        eout[:, cols] = dot(act[...], wout[:, cols]).astype(BF)
        return c

    lax.fori_loop(0, width // wtile, out_proj, 0)
    send_all(2, eout, rout)

    recv_all(1, sgrad, gsent)

    def backward(j, c):
        cols = pl.ds(pl.multiple_of(j * tile, tile), tile)
        gact = dot_nt(gsent[...], wout[cols, :])
        gpre[:, cols] = (gact * dgel[:, cols]).astype(BF)
        return c

    lax.fori_loop(0, hidden // tile, backward, 0)
    xt[0] = gsent[...].T

    def hop(m, d, t):
        return pltpu.make_async_remote_copy(
            src_ref=ring.at[m, d, t],
            dst_ref=ring.at[m, d, t + 1],
            send_sem=rsend.at[m, d, t],
            recv_sem=rrecv.at[m, d, t + 1],
            device_id={"dp": (up, down)[d]},
            device_id_type=MESH,
        )

    def arrived(m, d, t):
        pltpu.make_async_remote_copy(
            src_ref=ring.at[m, d, t],
            dst_ref=ring.at[m, d, t],
            send_sem=rsend.at[m, d, t - 1],
            recv_sem=rrecv.at[m, d, t],
            device_id={"dp": (up, down)[d]},
            device_id_type=MESH,
        ).wait_recv()

    def local_part(m, d, t):
        b = (z + nz - 1 - t) % nz if d == 0 else (z + 1 + t) % nz
        left = xt[m, pl.ds(pl.multiple_of(b * blk, blk), blk), :]
        other = (act, gpre)[m]
        return dot(left, other[:, d * half : (d + 1) * half])

    for m in (0, 1):
        for d in (0, 1):
            ring[m, d, 0] = local_part(m, d, 0).astype(BF)
            hop(m, d, 0).start()

    def grad_tokens(j, c):
        cols = pl.ds(pl.multiple_of(j * wtile, wtile), wtile)
        gtak[:, cols] = dot_nt(gpre[...], win[cols, :]).astype(BF)
        return c

    lax.fori_loop(0, width // wtile, grad_tokens, 0)
    send_all(3, gtak, rgrad)

    def ring_step(t, c):
        for m in (0, 1):
            for d in (0, 1):
                part[...] = local_part(m, d, t)
                arrived(m, d, t)
                ring[m, d, t] = (part[...] + ring[m, d, t].astype(F32)).astype(BF)
                hop(m, d, t).start()
        return c

    middle = min(5, nz - 1)
    lax.fori_loop(1, middle, ring_step, 0)

    recv_all(2, eout, rout)
    hi = gate_row.astype(BF).astype(F32)
    mixed[...] = (
        dot(jnp.where(selt, hi, 0.0).astype(BF), rout[...])
        + dot(jnp.where(selt, gate_row - hi, 0.0).astype(BF), rout[...])
    ).astype(BF)
    recv_all(3, gtak, rgrad)
    tgrad[...] = dot(selt.astype(F32).astype(BF), rgrad[...]).astype(BF)

    lax.fori_loop(middle, nz - 1, ring_step, 0)

    keep = pl.multiple_of(yh * half_rows, half_rows)
    give = pl.multiple_of((1 - yh) * half_rows, half_rows)

    def swap(m, d):
        return pltpu.make_async_remote_copy(
            src_ref=ysend.at[m, d],
            dst_ref=yrecv.at[m, d],
            send_sem=ysem_s.at[m, d],
            recv_sem=ysem_r.at[m, d],
            device_id={"dp": across},
            device_id_type=MESH,
        )

    for m in (0, 1):
        for d in (0, 1):
            part[...] = local_part(m, d, nz - 1)
            arrived(m, d, nz - 1)
            part[...] = part[...] + ring[m, d, nz - 1].astype(F32)
            ysend[m, d] = part[pl.ds(give, half_rows), :].astype(BF)
            swap(m, d).start()
            out = (gout, gin)[m]
            out[:, d * half : (d + 1) * half] = part[pl.ds(keep, half_rows), :].astype(BF)
    for m in (0, 1):
        for d in (0, 1):
            swap(m, d).wait()
            out = (gout, gin)[m]
            cols = slice(d * half, (d + 1) * half)
            out[:, cols] = (out[:, cols].astype(F32) + yrecv[m, d].astype(F32)).astype(BF)

    for which, src, dst in ((0, stok, taken), (1, sgrad, gsent), (2, eout, rout), (3, gtak, rgrad)):
        sent_all(which, src, dst)

    def ring_sent(t, c):
        for m in (0, 1):
            for d in (0, 1):
                hop(m, d, t).wait_send()
        return c

    lax.fori_loop(0, nz - 1, ring_sent, 0)


def on_device(n_dp, n_ex, tokens, picks, gates, w_in, w_out, cotangent):
    count, width = tokens.shape
    hidden = w_in.shape[2]
    per = picks.shape[2]
    rows = n_ex * per
    nz = n_dp // 2
    blk = width // nz
    half = hidden // 2
    vmem = pl.BlockSpec(memory_space=pltpu.VMEM)
    hbm = pl.BlockSpec(memory_space=pl.ANY)
    mixed, tgrad, gin, gout = pl.pallas_call(
        functools.partial(kernel, n_dp, n_ex),
        out_shape=(
            jax.ShapeDtypeStruct((count, width), BF),
            jax.ShapeDtypeStruct((count, width), BF),
            jax.ShapeDtypeStruct((width // n_dp, hidden), BF),
            jax.ShapeDtypeStruct((width // n_dp, hidden), BF),
        ),
        in_specs=[vmem, vmem, vmem, hbm, hbm, vmem],
        out_specs=(vmem, vmem, vmem, vmem),
        scratch_shapes=[
            pltpu.VMEM((width, hidden), BF),
            pltpu.VMEM((hidden, width), BF),
            pltpu.VMEM((rows, width), BF),
            pltpu.VMEM((rows, width), BF),
            pltpu.VMEM((rows, width), BF),
            pltpu.VMEM((rows, width), BF),
            pltpu.VMEM((rows, hidden), BF),
            pltpu.VMEM((rows, hidden), F32),
            pltpu.VMEM((rows, hidden), BF),
            pltpu.VMEM((rows, width), BF),
            pltpu.VMEM((rows, width), BF),
            pltpu.VMEM((rows, width), BF),
            pltpu.VMEM((rows, width), BF),
            pltpu.VMEM((2, width, rows), BF),
            pltpu.VMEM((blk, half), F32),
            pltpu.VMEM((2, 2, nz, blk, half), BF),
            pltpu.VMEM((2, 2, blk // 2, half), BF),
            pltpu.VMEM((2, 2, blk // 2, half), BF),
            pltpu.SemaphoreType.DMA((2,)),
            pltpu.SemaphoreType.DMA((4, n_ex)),
            pltpu.SemaphoreType.DMA((4, n_ex)),
            pltpu.SemaphoreType.DMA((2, 2, nz)),
            pltpu.SemaphoreType.DMA((2, 2, nz)),
            pltpu.SemaphoreType.DMA((2, 2)),
            pltpu.SemaphoreType.DMA((2, 2)),
        ],
        compiler_params=pltpu.CompilerParams(
            collective_id=0, has_side_effects=True, vmem_limit_bytes=58 * 1024 * 1024
        ),
        cost_estimate=pl.CostEstimate(
            flops=12 * rows * width * hidden,
            bytes_accessed=4 * width * hidden + 8 * count * width,
            transcendentals=2 * rows * hidden,
        ),
    )(tokens, picks, gates, w_in, w_out, cotangent)
    return mixed, tgrad, gin[:, None, :], gout[:, None, :]


def solution(mesh):
    n_dp, n_ex = mesh.shape["dp"], mesh.shape["expert"]
    in_specs = (
        P(("dp", "expert"), None),
        P(("dp", "expert"), None, None),
        P(("dp", "expert"), None, None),
        P("expert", None, None),
        P("expert", None, None),
        P(("dp", "expert"), None),
    )
    out_specs = (
        P(("dp", "expert"), None),
        P(("dp", "expert"), None),
        P("dp", "expert", None),
        P("dp", "expert", None),
    )
    return jax.shard_map(
        functools.partial(on_device, n_dp, n_ex),
        mesh=mesh,
        in_specs=in_specs,
        out_specs=out_specs,
        check_vma=False,
    )
```

time: 520 us -> 142 us (0.27)
  waiting for transfers between devices: 367 us -> 0 us
  Pallas kernels: 0 us -> 134 us
  matrix products: 59.2 us -> 0 us
  local copies, waits for them, and re-layouts: 32.9 us -> 7.07 us
  starting transfers between devices: 25.1 us -> 0 us
  other arithmetic: 16.7 us -> 0 us
  between operations: 14.8 us -> 0.64 us
    unnamed x2 -> x0, waiting for transfers between devices: 326 us -> none
    pallas_call x0 -> x1, Pallas kernels: none -> 134 us  [on_device(): pl.pallas_call(functools.partial(kernel, n_dp, n_ex), out_shape=(jax.Shap...]
    dot_general x7 -> x0, matrix products: 59.2 us -> none  [the longest x1 14.6 us: on_device(): jnp.einsum('seph,ehd->sepd', activated, w_out, preferred_element_type=jnp...]
    all_to_all x4 -> x0, waiting for transfers between devices: 41.5 us -> none  [the longest x1 13.1 us: on_device(): lax.all_to_all(expert_out.reshape(experts, per_pick, width), 'expert', sp...]
    all_to_all x4 -> x0, starting transfers between devices: 25.1 us -> none  [the longest x1 7.37 us: on_device(): lax.all_to_all(grad_sent, 'expert', split_axis=0, concat_axis=0, tiled=True)]
    concatenate x1 -> x0, local copies, waits for them, and re-layouts: 21.5 us -> none  [on_device(): jnp.concatenate([jnp.einsum('sepd,seph->deh', grouped, grad_pre, preferre...]
    concatenate x1 -> x0, other arithmetic: 6.19 us -> none  [on_device(): jnp.concatenate([jnp.einsum('sepd,seph->deh', grouped, grad_pre, preferre...]
    scatter-add x1 -> x0, other arithmetic: 5.88 us -> none  [on_device(): mixed = jnp.zeros((local_tokens, width), jnp.float32).at[flat_index].add(...]
  transfers between devices with their start and end apart: 5 -> 0, of which waited for: 5 -> 0; matrix products, arithmetic and copies ran while one was open for 8% -> 0% of each run, Pallas kernels for 0% -> 0%
where the time goes in v1:
time: 142 us; the launch traced here: 141 us
  Pallas kernels  134 us (94%)
  local copies, waits for them, and re-layouts  7.07 us (5%)
    pallas_call x1, Pallas kernels, on_device(): pl.pallas_call(functools.partial(kernel, n_dp, n_ex), out_shape=(jax.Shap...  134 us
    unnamed x4, local copies, waits for them, and re-layouts  7.07 us

profile of v1, /device:TPU:4, one launch (start us, length us, event | category | flops | bytes accessed | tf_op | source)
XLA Modules:
  0.0 141.3 jit_solution(14049744280354600871)
XLA Ops:
  0.6 133.6 %shard_map.93 = (bf16[256,1024]{1,0:T(8,128)(2,1)}, bf16[256,1024]{1,0:T(8,128)(2,1)}, bf16[64,2048]{1,0:T(8,128)(2,1)}, bf16[64,2048]{1,0:T(8,128)(2,1)}) custom-call(bf16[256,1024]{1,0:T(8,128)(2,1)} %tok.1, s32[1,16,32]{2,1,0:T(8,128)} %pick.1, f32[1,16,32]{2,1,0:T(8,128)} %gate.1, bf16[1,1024,2048]{2,1,0:T(8,128)(2,1)} %win_hbm.1, ...), custom_call_target="tpu_custom_call" | custom-call | flops 12884901888 | bytes 10485760 | tf_op jit(solution)/shard_map/pallas_call | solution.py:297
  134.2 1.9 %copy.14 = bf16[256,1024]{1,0:T(8,128)(2,1)} copy(bf16[256,1024]{1,0:T(8,128)(2,1)} %get-tuple-element.16) | data formatting | bytes 1048576
  136.1 1.9 %copy.15 = bf16[256,1024]{1,0:T(8,128)(2,1)} copy(bf16[256,1024]{1,0:T(8,128)(2,1)} %get-tuple-element.17) | data formatting | bytes 1048576
  138.0 1.7 %copy.16 = bf16[64,1,2048]{2,0,1:T(8,128)(2,1)} copy(bf16[64,1,2048]{2,0,1:T(8,128)(2,1)} %bitcast.3) | data formatting | bytes 524288
  139.6 1.7 %copy.17 = bf16[64,1,2048]{2,0,1:T(8,128)(2,1)} copy(bf16[64,1,2048]{2,0,1:T(8,128)(2,1)} %bitcast.2) | data formatting | bytes 524288

commit v2 on v1

v2 whole, which is shorter than its diff:
```python
import functools

import jax
import jax.numpy as jnp
from jax import lax
from jax.experimental import pallas as pl
from jax.experimental.pallas import tpu as pltpu
from jax.sharding import PartitionSpec as P

MESH = pl.DeviceIdType.MESH
BF = jnp.bfloat16
F32 = jnp.float32
NT = (((1,), (1,)), ((), ()))
ZC = 4


def dot(a, b):
    return jnp.dot(a, b, preferred_element_type=F32)


def dot_nt(a, b):
    return lax.dot_general(a, b, NT, preferred_element_type=F32)


def kernel(
    n_dp, n_ex, zc,
    tok_hbm, pick, gate, win_hbm, wout_hbm, cot_hbm,
    mixed, tgrad, gin, gout,
    win, wout, tok, cot, stok, sgrad, taken, gsent, gflat, act, dgel, gpre, eout, gtak, rout, rgrad,
    xt, part, ring_o, ring_i, ring_y, ykeep, ysend, yrecv,
    fin_o, fin_i, swap_so, swap_ro, swap_si, swap_ri,
    wsem, tsend, trecv, gsend, grecv,
    osend, orecv, isend, irecv, rysend, ryrecv, xsend, xrecv,
    sosend, sorecv, sisend, sirecv,
):
    nz = n_dp // 2
    tokens, width = tok.shape
    per = pick.shape[2]
    rows = n_ex * per
    hidden = win.shape[1]
    blk = width // nz
    half_rows = blk // 2
    half = hidden // 2
    yc = half - zc
    r = lax.axis_index("dp")
    me = lax.axis_index("expert")
    z = r // 2
    yh = r % 2
    up = (r + 2) % n_dp
    down = (r + n_dp - 2) % n_dp
    across = r + 1 - 2 * yh

    loads = [
        pltpu.make_async_copy(src, dst, wsem.at[i])
        for i, (src, dst) in enumerate(
            ((tok_hbm, tok), (cot_hbm, cot), (win_hbm.at[0], win), (wout_hbm.at[0], wout))
        )
    ]
    for load in loads:
        load.start()

    barrier = pltpu.get_barrier_semaphore()

    def greet(k, c):
        pl.semaphore_signal(
            barrier, inc=1, device_id={"expert": (me + k) % n_ex}, device_id_type=MESH
        )
        return c

    lax.fori_loop(1, n_ex, greet, 0)
    for other in (up, down, across):
        pl.semaphore_signal(barrier, inc=1, device_id={"dp": other}, device_id_type=MESH)

    p2 = pick[0].astype(F32).astype(BF)
    g = gate[0]
    g1 = g.astype(BF)
    g2 = (g - g1.astype(F32)).astype(BF)
    g3 = (g - g1.astype(F32) - g2.astype(F32)).astype(BF)
    row_e = lax.broadcasted_iota(jnp.int32, (rows, n_ex), 0) // per
    expert_of = (row_e == lax.broadcasted_iota(jnp.int32, (rows, n_ex), 1)).astype(F32).astype(BF)
    place = lax.broadcasted_iota(jnp.int32, (rows, per), 0) % per
    here = place == lax.broadcasted_iota(jnp.int32, (rows, per), 1)

    def column(values):
        return jnp.sum(jnp.where(here, values, 0.0), axis=1, keepdims=True)

    pick_col = column(dot(expert_of, p2))
    lanes = lax.broadcasted_iota(jnp.int32, (rows, tokens), 1).astype(F32)
    sel = (lanes == pick_col).astype(F32).astype(BF)
    loads[0].wait()
    stok[...] = dot(sel, tok[...]).astype(BF)

    def block_at(q):
        if q == nz - 1:
            return z
        if q == nz - 2:
            return (z + nz // 2) % nz
        return (z + 1 + q // 2) % nz if q % 2 else (z + nz - 1 - q // 2) % nz

    def order(d, t):
        if t == nz - 1:
            return nz - 1
        if t == nz // 2 - 1:
            return nz - 2
        if t < nz // 2:
            return 2 * t + d
        return 2 * (nz - 1 - t) - 1 - d

    def late(d, t):
        return 2 * (nz - 1 - t) - 1 - d

    def lane_block(b):
        return pl.ds(pl.multiple_of(b * blk, blk), blk)

    pl.semaphore_wait(barrier, n_ex + 2)

    def exchange(which, src, dst, peer, slot):
        return pltpu.make_async_remote_copy(
            src_ref=src.at[pl.ds(peer * per, per)],
            dst_ref=dst.at[pl.ds(slot * per, per)],
            send_sem=tsend.at[which, peer],
            recv_sem=trecv.at[which, slot],
            device_id={"expert": peer},
            device_id_type=MESH,
        )

    def peer_of(i):
        return (me + n_ex // 2 + (1 + i // 2) * (1 - 2 * (i % 2)) + n_ex) % n_ex

    def send_all(which, src, dst):
        exchange(which, src, dst, (me + n_ex // 2) % n_ex, me).start()

        def body(i, c):
            exchange(which, src, dst, peer_of(i), me).start()
            return c

        lax.fori_loop(0, n_ex - 2, body, 0)
        own = pl.ds(me * per, per)
        dst[own, :] = src[own, :]

    def recv_all(which, src, dst):
        def body(k, c):
            peer = (me + k) % n_ex
            exchange(which, src, dst, peer, peer).wait_recv()
            return c

        lax.fori_loop(1, n_ex, body, 0)

    def sent_all(which, src, dst):
        def body(k, c):
            exchange(which, src, dst, (me + k) % n_ex, me).wait_send()
            return c

        lax.fori_loop(1, n_ex, body, 0)

    def grad_chunk(i, peer, slot):
        return pltpu.make_async_remote_copy(
            src_ref=sgrad.at[pl.ds(2 * i, 2), pl.ds(peer * per, per)],
            dst_ref=gsent.at[pl.ds(2 * i, 2), pl.ds(slot * per, per)],
            send_sem=gsend.at[i, peer],
            recv_sem=grecv.at[i, slot],
            device_id={"expert": peer},
            device_id_type=MESH,
        )

    def send_grads(i, c):
        grad_chunk(i, (me + n_ex // 2) % n_ex, me).start()

        def body(k, c):
            grad_chunk(i, peer_of(k), me).start()
            return c

        lax.fori_loop(0, n_ex - 2, body, 0)
        return c

    def recv_grads(i):
        def body(k, c):
            peer = (me + k) % n_ex
            grad_chunk(i, peer, peer).wait_recv()
            return c

        lax.fori_loop(1, n_ex, body, 0)

    send_all(0, stok, taken)
    gate_col = column(dot(expert_of, g1) + dot(expert_of, g2) + dot(expert_of, g3))
    loads[1].wait()
    for q in range(nz):
        sgrad[q] = (dot(sel, cot[:, lane_block(block_at(q))]) * gate_col).astype(BF)
    lax.fori_loop(0, nz // 2, send_grads, 0)
    mine = pl.ds(me * per, per)
    for q in range(nz):
        gsent[q, mine, :] = sgrad[q, mine, :]

    here_bf = here.astype(F32).astype(BF)
    own_e = lax.broadcasted_iota(jnp.int32, (n_ex, rows), 0) == (
        lax.broadcasted_iota(jnp.int32, (n_ex, rows), 1) // per
    )

    def as_row(values):
        return jnp.sum(jnp.where(own_e, values, 0.0), axis=0, keepdims=True)

    pick_row = as_row(dot_nt(p2, here_bf))
    gate_row = as_row(dot_nt(g1, here_bf) + dot_nt(g2, here_bf) + dot_nt(g3, here_bf))

    tile = min(256, hidden)
    wtile = min(256, width)

    def forward(j, c):
        cols = pl.ds(pl.multiple_of(j * tile, tile), tile)
        pre = dot(taken[...], win[:, cols])
        cdf = 0.5 * (1.0 + lax.erf(pre * 0.7071067811865476))
        act[:, cols] = (pre * cdf).astype(BF)
        dgel[:, cols] = cdf + pre * (0.3989422804014327 * jnp.exp(-0.5 * pre * pre))
        return c

    def out_proj(j, c):
        cols = pl.ds(pl.multiple_of(j * wtile, wtile), wtile)
        eout[:, cols] = dot(act[...], wout[:, cols]).astype(BF)
        return c

    def backward(j, c):
        cols = pl.ds(pl.multiple_of(j * tile, tile), tile)
        gact = dot_nt(gflat[...], wout[cols, :])
        gpre[:, cols] = (gact * dgel[:, cols]).astype(BF)
        return c

    def grad_tokens(j, c):
        cols = pl.ds(pl.multiple_of(j * wtile, wtile), wtile)
        gtak[:, cols] = dot_nt(gpre[...], win[cols, :]).astype(BF)
        return c

    def hop(ring, ssem, rsem, d, j, t):
        return pltpu.make_async_remote_copy(
            src_ref=ring.at[d, j, t],
            dst_ref=ring.at[d, j, t + 1],
            send_sem=ssem.at[d, j, t],
            recv_sem=rsem.at[d, j, t + 1],
            device_id={"dp": (up, down)[d]},
            device_id_type=MESH,
        )

    def arrived(ring, ssem, rsem, d, j, t):
        pltpu.make_async_remote_copy(
            src_ref=ring.at[d, j, t],
            dst_ref=ring.at[d, j, t],
            send_sem=ssem.at[d, j, t - 1],
            recv_sem=rsem.at[d, j, t],
            device_id={"dp": (up, down)[d]},
            device_id_type=MESH,
        ).wait_recv()

    def block_of(d, t):
        return (z + nz - 1 - t) % nz if d == 0 else (z + 1 + t) % nz

    def out_part(q, c0, n):
        return dot(gsent[q].T, act[:, c0 : c0 + n])

    def in_part(d, t):
        left = xt[pl.ds(pl.multiple_of(block_of(d, t) * blk, blk), blk), :]
        return dot(left, gpre[:, d * half : (d + 1) * half])

    out_set = (ring_o, osend, orecv)
    in_set = (ring_i, isend, irecv)
    y_set = (ring_y, rysend, ryrecv)

    def pass_on(which, n, d, t, first=False):
        ring = which[0]
        w = n // 2
        for j in (0, 1):
            value = part[d, :, j * w : (j + 1) * w]
            if not first:
                arrived(*which, d, j, t)
                value = value + ring[d, j, t].astype(F32)
            ring[d, j, t] = value.astype(BF)
            hop(*which, d, j, t).start()

    def out_step(t, q):
        for d in (0, 1):
            part[d, :, :zc] = out_part(q[d], d * zc, zc)
        for d in (0, 1):
            pass_on(out_set, zc, d, t, first=isinstance(t, int) and t == 0)

    def in_step(t, ds=(0, 1)):
        for d in ds:
            part[d, :, :half] = in_part(d, t)
        for d in ds:
            pass_on(in_set, half, d, t, first=isinstance(t, int) and t == 0)

    keep = pl.multiple_of(yh * half_rows, half_rows)
    give = pl.multiple_of((1 - yh) * half_rows, half_rows)

    def swap(sbuf, rbuf, ssem, rsem, d, j):
        return pltpu.make_async_remote_copy(
            src_ref=sbuf.at[d, j],
            dst_ref=rbuf.at[d, j],
            send_sem=ssem.at[d, j],
            recv_sem=rsem.at[d, j],
            device_id={"dp": across},
            device_id_type=MESH,
        )

    out_swap = (swap_so, swap_ro, sosend, sorecv)
    in_swap = (swap_si, swap_ri, sisend, sirecv)

    def last_step(which, swapping, fin, n, fill):
        w = n // 2
        for d in (0, 1):
            part[d, :, :n] = fill(d)
        for d in (0, 1):
            for j in (0, 1):
                arrived(*which, d, j, nz - 1)
                cols = slice(j * w, (j + 1) * w)
                part[d, :, cols] = part[d, :, cols] + which[0][d, j, nz - 1].astype(F32)
                swapping[0][d, j] = part[d, pl.ds(give, half_rows), cols].astype(BF)
                swap(*swapping, d, j).start()
                fin[d, j] = part[d, pl.ds(keep, half_rows), cols]

    def finish(swapping, fin, n, out, base):
        w = n // 2
        for d in (0, 1):
            for j in (0, 1):
                swap(*swapping, d, j).wait()
                c0 = base + d * n + j * w
                out[:, c0 : c0 + w] = (fin[d, j] + swapping[1][d, j].astype(F32)).astype(BF)

    def across_copy(d, t):
        return pltpu.make_async_remote_copy(
            src_ref=ysend.at[d, t],
            dst_ref=yrecv.at[d, t],
            send_sem=xsend.at[d, t],
            recv_sem=xrecv.at[d, t],
            device_id={"dp": across},
            device_id_type=MESH,
        )

    def y_part(t, q):
        for d in (0, 1):
            part[d, :, :yc] = out_part(q[d], 2 * zc + d * yc, yc)
            ysend[d, t] = part[d, pl.ds(give, half_rows), :yc].astype(BF)
            across_copy(d, t).start()
            ykeep[d, t] = part[d, pl.ds(keep, half_rows), :yc]

    def y_step(t, first=False, last=False):
        w = yc // 2
        for d in (0, 1):
            across_copy(d, t).wait_recv()
            for j in (0, 1):
                cols = slice(j * w, (j + 1) * w)
                value = ykeep[d, t, :, cols] + yrecv[d, t, :, cols].astype(F32)
                if not first:
                    arrived(*y_set, d, j, t)
                    value = value + ring_y[d, j, t].astype(F32)
                if last:
                    c0 = 2 * zc + d * yc + j * w
                    gout[:, c0 : c0 + w] = value.astype(BF)
                else:
                    ring_y[d, j, t] = value.astype(BF)
                    hop(*y_set, d, j, t).start()

    def both(t):
        return (order(0, t), order(1, t))

    loads[2].wait()
    recv_all(0, stok, taken)
    first_tiles = 2 * zc // tile
    lax.fori_loop(0, first_tiles, forward, 0)
    recv_grads(0)
    out_step(0, both(0))
    lax.fori_loop(first_tiles, hidden // tile, forward, 0)
    y_part(0, both(0))
    recv_grads(1)
    out_step(1, both(1))
    y_part(1, both(1))
    loads[3].wait()
    xt[...] = taken[...].T
    lax.fori_loop(0, width // wtile // 2, out_proj, 0)
    recv_grads(2)
    out_step(2, both(2))
    y_part(2, both(2))
    lax.fori_loop(width // wtile // 2, width // wtile, out_proj, 0)
    recv_grads(3)
    for q in range(nz):
        gflat[:, lane_block(block_at(q))] = gsent[q]
    out_step(3, both(3))
    lax.fori_loop(0, hidden // tile // 2, backward, 0)
    in_step(0, (0,))
    lax.fori_loop(hidden // tile // 2, hidden // tile, backward, 0)
    in_step(0, (1,))
    y_part(3, both(3))

    def y_late(t, c):
        y_part(t, (late(0, t), late(1, t)))
        return c

    lax.fori_loop(4, nz - 1, y_late, 0)
    y_part(nz - 1, both(nz - 1))
    out_step(4, both(4))
    send_all(1, eout, rout)
    lax.fori_loop(0, width // wtile, grad_tokens, 0)
    in_step(1)
    send_all(2, gtak, rgrad)

    def middle(t, c):
        out_step(t, (late(0, t), late(1, t)))
        in_step(t - 3)
        return c

    lax.fori_loop(5, nz - 1, middle, 0)
    last_step(out_set, out_swap, fin_o, zc, lambda d: out_part(nz - 1, d * zc, zc))
    y_step(0, first=True)
    in_step(4)

    def steady(t, c):
        y_step(t)
        in_step(t + 4)
        return c

    lax.fori_loop(1, nz - 5, steady, 0)

    finish(out_swap, fin_o, zc, gout, 0)
    recv_all(1, eout, rout)
    selt = lax.broadcasted_iota(jnp.int32, (tokens, rows), 0).astype(F32) == pick_row
    hi = gate_row.astype(BF).astype(F32)
    mixed[...] = (
        dot(jnp.where(selt, hi, 0.0).astype(BF), rout[...])
        + dot(jnp.where(selt, gate_row - hi, 0.0).astype(BF), rout[...])
    ).astype(BF)
    recv_all(2, gtak, rgrad)
    tgrad[...] = dot(selt.astype(F32).astype(BF), rgrad[...]).astype(BF)

    y_step(3)
    last_step(in_set, in_swap, fin_i, half, lambda d: in_part(d, nz - 1))

    def tail(t, c):
        y_step(t)
        return c

    lax.fori_loop(4, nz - 1, tail, 0)
    finish(in_swap, fin_i, half, gin, 0)
    y_step(nz - 1, last=True)

    for which, src, dst in ((0, stok, taken), (1, eout, rout), (2, gtak, rgrad)):
        sent_all(which, src, dst)

    def grads_gone(i, c):
        def body(k, c):
            grad_chunk(i, (me + k) % n_ex, me).wait_send()
            return c

        lax.fori_loop(1, n_ex, body, 0)
        return c

    lax.fori_loop(0, nz // 2, grads_gone, 0)

    def ring_sent(t, c):
        for d in (0, 1):
            for j in (0, 1):
                for which in (out_set, in_set, y_set):
                    hop(*which, d, j, t).wait_send()
        return c

    lax.fori_loop(0, nz - 1, ring_sent, 0)

    def across_sent(t, c):
        for d in (0, 1):
            across_copy(d, t).wait_send()
        return c

    lax.fori_loop(0, nz, across_sent, 0)


def deliver(*refs):
    sem = refs[-1]
    count = len(refs) // 2
    copies = [
        pltpu.make_async_copy(refs[i], refs[count + i], sem.at[i]) for i in range(count)
    ]
    for copy in copies:
        copy.start()
    for copy in copies:
        copy.wait()


def on_device(n_dp, n_ex, tokens, picks, gates, w_in, w_out, cotangent):
    count, width = tokens.shape
    hidden = w_in.shape[2]
    per = picks.shape[2]
    rows = n_ex * per
    nz = n_dp // 2
    blk = width // nz
    half = hidden // 2
    zc = half * ZC // 8
    yc = half - zc
    vmem = pl.BlockSpec(memory_space=pltpu.VMEM)
    hbm = pl.BlockSpec(memory_space=pl.ANY)
    dma = pltpu.SemaphoreType.DMA
    results = pl.pallas_call(
        functools.partial(kernel, n_dp, n_ex, zc),
        out_shape=(
            jax.ShapeDtypeStruct((count, width), BF),
            jax.ShapeDtypeStruct((count, width), BF),
            jax.ShapeDtypeStruct((width // n_dp, hidden), BF),
            jax.ShapeDtypeStruct((width // n_dp, hidden), BF),
        ),
        in_specs=[hbm, vmem, vmem, hbm, hbm, hbm],
        out_specs=(vmem, vmem, vmem, vmem),
        scratch_shapes=[
            pltpu.VMEM((width, hidden), BF),
            pltpu.VMEM((hidden, width), BF),
            pltpu.VMEM((count, width), BF),
            pltpu.VMEM((count, width), BF),
            pltpu.VMEM((rows, width), BF),
            pltpu.VMEM((nz, rows, blk), BF),
            pltpu.VMEM((rows, width), BF),
            pltpu.VMEM((nz, rows, blk), BF),
            pltpu.VMEM((rows, width), BF),
            pltpu.VMEM((rows, hidden), BF),
            pltpu.VMEM((rows, hidden), F32),
            pltpu.VMEM((rows, hidden), BF),
            pltpu.VMEM((rows, width), BF),
            pltpu.VMEM((rows, width), BF),
            pltpu.VMEM((rows, width), BF),
            pltpu.VMEM((rows, width), BF),
            pltpu.VMEM((width, rows), BF),
            pltpu.VMEM((2, blk, half), F32),
            pltpu.VMEM((2, 2, nz, blk, zc // 2), BF),
            pltpu.VMEM((2, 2, nz, blk, half // 2), BF),
            pltpu.VMEM((2, 2, nz, blk // 2, yc // 2), BF),
            pltpu.VMEM((2, nz, blk // 2, yc), F32),
            pltpu.VMEM((2, nz, blk // 2, yc), BF),
            pltpu.VMEM((2, nz, blk // 2, yc), BF),
            pltpu.VMEM((2, 2, blk // 2, zc // 2), F32),
            pltpu.VMEM((2, 2, blk // 2, half // 2), F32),
            pltpu.VMEM((2, 2, blk // 2, zc // 2), BF),
            pltpu.VMEM((2, 2, blk // 2, zc // 2), BF),
            pltpu.VMEM((2, 2, blk // 2, half // 2), BF),
            pltpu.VMEM((2, 2, blk // 2, half // 2), BF),
            dma((4,)),
            dma((3, n_ex)),
            dma((3, n_ex)),
            dma((nz // 2, n_ex)),
            dma((nz // 2, n_ex)),
            dma((2, 2, nz)),
            dma((2, 2, nz)),
            dma((2, 2, nz)),
            dma((2, 2, nz)),
            dma((2, 2, nz)),
            dma((2, 2, nz)),
            dma((2, nz)),
            dma((2, nz)),
            dma((2, 2)),
            dma((2, 2)),
            dma((2, 2)),
            dma((2, 2)),
        ],
        compiler_params=pltpu.CompilerParams(
            collective_id=0, has_side_effects=True, vmem_limit_bytes=58 * 1024 * 1024
        ),
        cost_estimate=pl.CostEstimate(
            flops=12 * rows * width * hidden,
            bytes_accessed=4 * width * hidden + 8 * count * width,
            transcendentals=2 * rows * hidden,
        ),
    )(tokens, picks, gates, w_in, w_out, cotangent)
    mixed, tgrad, gin, gout = pl.pallas_call(
        deliver,
        out_shape=tuple(jax.ShapeDtypeStruct(a.shape, a.dtype) for a in results),
        in_specs=[vmem] * 4,
        out_specs=(hbm,) * 4,
        scratch_shapes=[dma((4,))],
        compiler_params=pltpu.CompilerParams(vmem_limit_bytes=58 * 1024 * 1024),
    )(*results)
    return mixed, tgrad, gin[:, None, :], gout[:, None, :]


def solution(mesh):
    n_dp, n_ex = mesh.shape["dp"], mesh.shape["expert"]
    in_specs = (
        P(("dp", "expert"), None),
        P(("dp", "expert"), None, None),
        P(("dp", "expert"), None, None),
        P("expert", None, None),
        P("expert", None, None),
        P(("dp", "expert"), None),
    )
    out_specs = (
        P(("dp", "expert"), None),
        P(("dp", "expert"), None),
        P("dp", "expert", None),
        P("dp", "expert", None),
    )
    return jax.shard_map(
        functools.partial(on_device, n_dp, n_ex),
        mesh=mesh,
        in_specs=in_specs,
        out_specs=out_specs,
        check_vma=False,
    )
```

time: 142 us -> 120 us (0.85)
  Pallas kernels: 134 us -> 119 us
  local copies, waits for them, and re-layouts: 7.07 us -> 0 us
    pallas_call x1 -> x2, Pallas kernels: 134 us -> 119 us  [the longest x1 116 us: on_device(): pl.pallas_call(functools.partial(kernel, n_dp, n_ex, zc), out_shape=(jax....]
    unnamed x4 -> x0, local copies, waits for them, and re-layouts: 7.07 us -> none
where the time goes in v2:
time: 120 us; the launch traced here: 119 us
  Pallas kernels  119 us (99%)
    pallas_call x1, Pallas kernels, on_device(): pl.pallas_call(functools.partial(kernel, n_dp, n_ex, zc), out_shape=(jax....  116 us
    pallas_call x1, Pallas kernels, on_device(): pl.pallas_call(deliver, out_shape=tuple((jax.ShapeDtypeStruct(a.shape, a....  2.51 us

profile of v2, /device:TPU:4, one launch (start us, length us, event | category | flops | bytes accessed | tf_op | source)
XLA Modules:
  0.0 119.4 jit_solution(8212702728610025741)
XLA Ops:
  0.6 116.3 %shard_map.93 = (bf16[256,1024]{1,0:T(8,128)(2,1)}, bf16[256,1024]{1,0:T(8,128)(2,1)}, bf16[64,2048]{1,0:T(8,128)(2,1)}, bf16[64,2048]{1,0:T(8,128)(2,1)}) custom-call(bf16[256,1024]{1,0:T(8,128)(2,1)} %tok_hbm.1, s32[1,16,32]{2,1,0:T(8,128)} %pick.1, f32[1,16,32]{2,1,0:T(8,128)} %gate.1, bf16[1,1024,2048]{2,1,0:T(8,128)(2,1)} %win_hbm.1, ...), custom_call_target="tpu_custom_call" | custom-call | flops 12884901888 | bytes 10485760 | tf_op jit(solution)/shard_map/pallas_call | solution.py:497
  116.9 2.5 %shard_map.94 = (bf16[256,1024]{1,0:T(8,128)(2,1)}, bf16[256,1024]{1,0:T(8,128)(2,1)}, bf16[64,2048]{1,0:T(8,128)(2,1)}, bf16[64,2048]{1,0:T(8,128)(2,1)}) custom-call(bf16[256,1024]{1,0:T(8,128)(2,1)} %get-tuple-element.12.refs_0_, bf16[256,1024]{1,0:T(8,128)(2,1)} %get-tuple-element.13.refs_1_, bf16[64,2048]{1,0:T(8,128)(2,1)} %get-tuple-element.14.refs_2_, ...), custom_call_target="tpu_custom_call" | custom-call | tf_op jit(solution)/shard_map/pallas_call | solution.py:565

commit v3 on v2

--- a/solution.py
+++ b/solution.py
@@ -12,6 +12,7 @@
 F32 = jnp.float32
 NT = (((1,), (1,)), ((), ()))
 ZC = 4
+SUBS = (2, 2, 1)
 
 
 def dot(a, b):
@@ -93,21 +94,11 @@
     def block_at(q):
         if q == nz - 1:
             return z
-        if q == nz - 2:
-            return (z + nz // 2) % nz
-        return (z + 1 + q // 2) % nz if q % 2 else (z + nz - 1 - q // 2) % nz
-
-    def order(d, t):
-        if t == nz - 1:
-            return nz - 1
-        if t == nz // 2 - 1:
-            return nz - 2
-        if t < nz // 2:
-            return 2 * t + d
-        return 2 * (nz - 1 - t) - 1 - d
-
-    def late(d, t):
-        return 2 * (nz - 1 - t) - 1 - d
+        back = (q + 1) // 2
+        return (z + nz // 2 - back) % nz if q % 2 else (z + nz // 2 + back) % nz
+
+    def place_of(d, p):
+        return 0 if p == 0 else 2 * p - 1 + d
 
     def lane_block(b):
         return pl.ds(pl.multiple_of(b * blk, blk), blk)
@@ -153,17 +144,20 @@
 
         lax.fori_loop(1, n_ex, body, 0)
 
+    chunks = ((0, 1), (1, 2), (3, 2), (5, 3))
+
     def grad_chunk(i, peer, slot):
+        at = pl.ds(*chunks[i])
         return pltpu.make_async_remote_copy(
-            src_ref=sgrad.at[pl.ds(2 * i, 2), pl.ds(peer * per, per)],
-            dst_ref=gsent.at[pl.ds(2 * i, 2), pl.ds(slot * per, per)],
+            src_ref=sgrad.at[at, pl.ds(peer * per, per)],
+            dst_ref=gsent.at[at, pl.ds(slot * per, per)],
             send_sem=gsend.at[i, peer],
             recv_sem=grecv.at[i, slot],
             device_id={"expert": peer},
             device_id_type=MESH,
         )
 
-    def send_grads(i, c):
+    def send_grads(i):
         grad_chunk(i, (me + n_ex // 2) % n_ex, me).start()
 
         def body(k, c):
@@ -171,7 +165,6 @@
             return c
 
         lax.fori_loop(0, n_ex - 2, body, 0)
-        return c
 
     def recv_grads(i):
         def body(k, c):
@@ -186,7 +179,8 @@
     loads[1].wait()
     for q in range(nz):
         sgrad[q] = (dot(sel, cot[:, lane_block(block_at(q))]) * gate_col).astype(BF)
-    lax.fori_loop(0, nz // 2, send_grads, 0)
+    for i in range(len(chunks)):
+        send_grads(i)
     mine = pl.ds(me * per, per)
     for q in range(nz):
         gsent[q, mine, :] = sgrad[q, mine, :]
@@ -229,72 +223,79 @@
         gtak[:, cols] = dot_nt(gpre[...], win[cols, :]).astype(BF)
         return c
 
-    def hop(ring, ssem, rsem, d, j, t):
+    chains = ((0, 0, 0), (1, 1, 0), (0, 1, 1), (1, 0, 1))
+    hops = nz // 2
+
+    def hop(flow, c, j, t):
+        ring, ssem, rsem = flow
         return pltpu.make_async_remote_copy(
-            src_ref=ring.at[d, j, t],
-            dst_ref=ring.at[d, j, t + 1],
-            send_sem=ssem.at[d, j, t],
-            recv_sem=rsem.at[d, j, t + 1],
-            device_id={"dp": (up, down)[d]},
+            src_ref=ring.at[c, j, t],
+            dst_ref=ring.at[c, j, t + 1],
+            send_sem=ssem.at[c, j, t],
+            recv_sem=rsem.at[c, j, t + 1],
+            device_id={"dp": (up, down)[chains[c][1]]},
             device_id_type=MESH,
         )
 
-    def arrived(ring, ssem, rsem, d, j, t):
+    def arrived(flow, c, j, t):
+        ring, ssem, rsem = flow
         pltpu.make_async_remote_copy(
-            src_ref=ring.at[d, j, t],
-            dst_ref=ring.at[d, j, t],
-            send_sem=ssem.at[d, j, t - 1],
-            recv_sem=rsem.at[d, j, t],
-            device_id={"dp": (up, down)[d]},
+            src_ref=ring.at[c, j, t],
+            dst_ref=ring.at[c, j, t],
+            send_sem=ssem.at[c, j, t - 1],
+            recv_sem=rsem.at[c, j, t],
+            device_id={"dp": (up, down)[chains[c][1]]},
             device_id_type=MESH,
         ).wait_recv()
 
-    def block_of(d, t):
-        return (z + nz - 1 - t) % nz if d == 0 else (z + 1 + t) % nz
+    out_flow = (ring_o, osend, orecv)
+    in_flow = (ring_i, isend, irecv)
+    y_flow = (ring_y, rysend, ryrecv)
 
     def out_part(q, c0, n):
         return dot(gsent[q].T, act[:, c0 : c0 + n])
 
-    def in_part(d, t):
-        left = xt[pl.ds(pl.multiple_of(block_of(d, t) * blk, blk), blk), :]
-        return dot(left, gpre[:, d * half : (d + 1) * half])
-
-    out_set = (ring_o, osend, orecv)
-    in_set = (ring_i, isend, irecv)
-    y_set = (ring_y, rysend, ryrecv)
-
-    def pass_on(which, n, d, t, first=False):
-        ring = which[0]
-        w = n // 2
-        for j in (0, 1):
-            value = part[d, :, j * w : (j + 1) * w]
-            if not first:
-                arrived(*which, d, j, t)
-                value = value + ring[d, j, t].astype(F32)
-            ring[d, j, t] = value.astype(BF)
-            hop(*which, d, j, t).start()
-
-    def out_step(t, q):
-        for d in (0, 1):
-            part[d, :, :zc] = out_part(q[d], d * zc, zc)
-        for d in (0, 1):
-            pass_on(out_set, zc, d, t, first=isinstance(t, int) and t == 0)
-
-    def in_step(t, ds=(0, 1)):
-        for d in ds:
-            part[d, :, :half] = in_part(d, t)
-        for d in ds:
-            pass_on(in_set, half, d, t, first=isinstance(t, int) and t == 0)
+    def in_part(q, c0, n):
+        b = block_at(q)
+        left = xt[pl.ds(pl.multiple_of(b * blk, blk), blk), :]
+        return dot(left, gpre[:, c0 : c0 + n])
+
+    def pass_on(flow, c, t, values, w):
+        ring = flow[0]
+        subs = ring.shape[1]
+        v = w // subs
+        for j in range(subs):
+            value = values(slice(j * v, (j + 1) * v))
+            if t > 0:
+                arrived(flow, c, j, t)
+                value = value + ring[c, j, t].astype(F32)
+            ring[c, j, t] = value.astype(BF)
+            hop(flow, c, j, t).start()
+
+    def z_step(flow, product, w, t, which):
+        which = [c for c in which if t < hops - chains[c][2]]
+        for c in which:
+            h, d, p = chains[c]
+            part[c, :, :w] = product(place_of(d, t + p), h * w, w)
+        for c in which:
+            pass_on(flow, c, t, lambda cols, c=c: part[c, :, cols], w)
+
+    def out_step(t, which=(0, 1, 2, 3)):
+        z_step(out_flow, out_part, zc, t, which)
+
+    def in_step(t, which=(0, 1, 2, 3)):
+        z_step(in_flow, in_part, half, t, which)
 
     keep = pl.multiple_of(yh * half_rows, half_rows)
     give = pl.multiple_of((1 - yh) * half_rows, half_rows)
 
-    def swap(sbuf, rbuf, ssem, rsem, d, j):
+    def swap(swapping, h, j):
+        sbuf, rbuf, ssem, rsem = swapping
         return pltpu.make_async_remote_copy(
-            src_ref=sbuf.at[d, j],
-            dst_ref=rbuf.at[d, j],
-            send_sem=ssem.at[d, j],
-            recv_sem=rsem.at[d, j],
+            src_ref=sbuf.at[h, j],
+            dst_ref=rbuf.at[h, j],
+            send_sem=ssem.at[h, j],
+            recv_sem=rsem.at[h, j],
             device_id={"dp": across},
             device_id_type=MESH,
         )
@@ -302,122 +303,120 @@
     out_swap = (swap_so, swap_ro, sosend, sorecv)
     in_swap = (swap_si, swap_ri, sisend, sirecv)
 
-    def last_step(which, swapping, fin, n, fill):
-        w = n // 2
-        for d in (0, 1):
-            part[d, :, :n] = fill(d)
-        for d in (0, 1):
-            for j in (0, 1):
-                arrived(*which, d, j, nz - 1)
-                cols = slice(j * w, (j + 1) * w)
-                part[d, :, cols] = part[d, :, cols] + which[0][d, j, nz - 1].astype(F32)
-                swapping[0][d, j] = part[d, pl.ds(give, half_rows), cols].astype(BF)
-                swap(*swapping, d, j).start()
-                fin[d, j] = part[d, pl.ds(keep, half_rows), cols]
-
-    def finish(swapping, fin, n, out, base):
-        w = n // 2
-        for d in (0, 1):
-            for j in (0, 1):
-                swap(*swapping, d, j).wait()
-                c0 = base + d * n + j * w
-                out[:, c0 : c0 + w] = (fin[d, j] + swapping[1][d, j].astype(F32)).astype(BF)
-
-    def across_copy(d, t):
+    def both_arrived(flow, h, j):
+        long, short = h, 2 + h
+        arrived(flow, long, j, hops)
+        arrived(flow, short, j, hops - 1)
+        ring = flow[0]
+        return ring[long, j, hops].astype(F32) + ring[short, j, hops - 1].astype(F32)
+
+    def last_step(flow, product, swapping, fin, w):
+        subs = flow[0].shape[1]
+        v = w // subs
+        for h in (0, 1):
+            part[h, :, :w] = product(nz - 1, h * w, w)
+        for h in (0, 1):
+            for j in range(subs):
+                cols = slice(j * v, (j + 1) * v)
+                part[h, :, cols] = part[h, :, cols] + both_arrived(flow, h, j)
+                swapping[0][h, j] = part[h, pl.ds(give, half_rows), cols].astype(BF)
+                swap(swapping, h, j).start()
+                fin[h, j] = part[h, pl.ds(keep, half_rows), cols]
+
+    def finish(swapping, fin, w, out):
+        subs = fin.shape[1]
+        v = w // subs
+        for h in (0, 1):
+            for j in range(subs):
+                swap(swapping, h, j).wait()
+                c0 = h * w + j * v
+                out[:, c0 : c0 + v] = (fin[h, j] + swapping[1][h, j].astype(F32)).astype(BF)
+
+    def across_copy(q):
         return pltpu.make_async_remote_copy(
-            src_ref=ysend.at[d, t],
-            dst_ref=yrecv.at[d, t],
-            send_sem=xsend.at[d, t],
-            recv_sem=xrecv.at[d, t],
+            src_ref=ysend.at[q],
+            dst_ref=yrecv.at[q],
+            send_sem=xsend.at[q],
+            recv_sem=xrecv.at[q],
             device_id={"dp": across},
             device_id_type=MESH,
         )
 
-    def y_part(t, q):
-        for d in (0, 1):
-            part[d, :, :yc] = out_part(q[d], 2 * zc + d * yc, yc)
-            ysend[d, t] = part[d, pl.ds(give, half_rows), :yc].astype(BF)
-            across_copy(d, t).start()
-            ykeep[d, t] = part[d, pl.ds(keep, half_rows), :yc]
-
-    def y_step(t, first=False, last=False):
-        w = yc // 2
-        for d in (0, 1):
-            across_copy(d, t).wait_recv()
-            for j in (0, 1):
-                cols = slice(j * w, (j + 1) * w)
-                value = ykeep[d, t, :, cols] + yrecv[d, t, :, cols].astype(F32)
-                if not first:
-                    arrived(*y_set, d, j, t)
-                    value = value + ring_y[d, j, t].astype(F32)
-                if last:
-                    c0 = 2 * zc + d * yc + j * w
-                    gout[:, c0 : c0 + w] = value.astype(BF)
-                else:
-                    ring_y[d, j, t] = value.astype(BF)
-                    hop(*y_set, d, j, t).start()
-
-    def both(t):
-        return (order(0, t), order(1, t))
+    def y_part(q):
+        for h in (0, 1):
+            cols = slice(h * yc, (h + 1) * yc)
+            part[h, :, :yc] = out_part(q, 2 * zc + h * yc, yc)
+            ysend[q, :, cols] = part[h, pl.ds(give, half_rows), :yc].astype(BF)
+            ykeep[q, :, cols] = part[h, pl.ds(keep, half_rows), :yc]
+        across_copy(q).start()
+
+    def y_sum(q, h, cols):
+        at = slice(h * yc + cols.start, h * yc + cols.stop)
+        return ykeep[q, :, at] + yrecv[q, :, at].astype(F32)
+
+    def y_step(t):
+        for c in (0, 1, 2, 3):
+            h, d, p = chains[c]
+            if t < hops - p:
+                q = place_of(d, t + p)
+                if c >= 2 or q == 0 and c == 0:
+                    across_copy(q).wait_recv()
+                pass_on(y_flow, c, t, lambda cols, q=q, h=h: y_sum(q, h, cols), yc)
+
+    def y_last():
+        across_copy(nz - 1).wait_recv()
+        subs = ring_y.shape[1]
+        v = yc // subs
+        for h in (0, 1):
+            for j in range(subs):
+                value = y_sum(nz - 1, h, slice(j * v, (j + 1) * v)) + both_arrived(y_flow, h, j)
+                c0 = 2 * zc + h * yc + j * v
+                gout[:, c0 : c0 + v] = value.astype(BF)
 
     loads[2].wait()
     recv_all(0, stok, taken)
     first_tiles = 2 * zc // tile
+    all_tiles = hidden // tile
     lax.fori_loop(0, first_tiles, forward, 0)
     recv_grads(0)
-    out_step(0, both(0))
-    lax.fori_loop(first_tiles, hidden // tile, forward, 0)
-    y_part(0, both(0))
+    out_step(0, (0, 1))
+    middle_tile = (first_tiles + all_tiles) // 2
+    lax.fori_loop(first_tiles, middle_tile, forward, 0)
     recv_grads(1)
-    out_step(1, both(1))
-    y_part(1, both(1))
+    out_step(0, (2, 3))
+    lax.fori_loop(middle_tile, all_tiles, forward, 0)
+    for q in (0, 1, 2):
+        y_part(q)
+    out_step(1, (0, 1))
+    recv_grads(2)
+    out_step(1, (2, 3))
+    for q in (3, 4):
+        y_part(q)
     loads[3].wait()
     xt[...] = taken[...].T
-    lax.fori_loop(0, width // wtile // 2, out_proj, 0)
-    recv_grads(2)
-    out_step(2, both(2))
-    y_part(2, both(2))
-    lax.fori_loop(width // wtile // 2, width // wtile, out_proj, 0)
+    out_tiles = width // wtile
+    lax.fori_loop(0, out_tiles, out_proj, 0)
     recv_grads(3)
     for q in range(nz):
         gflat[:, lane_block(block_at(q))] = gsent[q]
-    out_step(3, both(3))
-    lax.fori_loop(0, hidden // tile // 2, backward, 0)
-    in_step(0, (0,))
-    lax.fori_loop(hidden // tile // 2, hidden // tile, backward, 0)
-    in_step(0, (1,))
-    y_part(3, both(3))
-
-    def y_late(t, c):
-        y_part(t, (late(0, t), late(1, t)))
-        return c
-
-    lax.fori_loop(4, nz - 1, y_late, 0)
-    y_part(nz - 1, both(nz - 1))
-    out_step(4, both(4))
+    out_step(2)
+    lax.fori_loop(0, all_tiles // 2, backward, 0)
+    in_step(0, (0, 2))
+    lax.fori_loop(all_tiles // 2, all_tiles, backward, 0)
+    in_step(0, (1, 3))
+    for q in (5, 6, 7):
+        y_part(q)
+    out_step(3)
     send_all(1, eout, rout)
-    lax.fori_loop(0, width // wtile, grad_tokens, 0)
+    lax.fori_loop(0, out_tiles, grad_tokens, 0)
+    send_all(2, gtak, rgrad)
     in_step(1)
-    send_all(2, gtak, rgrad)
-
-    def middle(t, c):
-        out_step(t, (late(0, t), late(1, t)))
-        in_step(t - 3)
-        return c
-
-    lax.fori_loop(5, nz - 1, middle, 0)
-    last_step(out_set, out_swap, fin_o, zc, lambda d: out_part(nz - 1, d * zc, zc))
-    y_step(0, first=True)
-    in_step(4)
-
-    def steady(t, c):
-        y_step(t)
-        in_step(t + 4)
-        return c
-
-    lax.fori_loop(1, nz - 5, steady, 0)
-
-    finish(out_swap, fin_o, zc, gout, 0)
+    y_step(0)
+    last_step(out_flow, out_part, out_swap, fin_o, zc)
+    in_step(2)
+    y_step(1)
+    in_step(3)
+
     recv_all(1, eout, rout)
     selt = lax.broadcasted_iota(jnp.int32, (tokens, rows), 0).astype(F32) == pick_row
     hi = gate_row.astype(BF).astype(F32)
@@ -428,42 +427,31 @@
     recv_all(2, gtak, rgrad)
     tgrad[...] = dot(selt.astype(F32).astype(BF), rgrad[...]).astype(BF)
 
+    y_step(2)
+    last_step(in_flow, in_part, in_swap, fin_i, half)
     y_step(3)
-    last_step(in_set, in_swap, fin_i, half, lambda d: in_part(d, nz - 1))
-
-    def tail(t, c):
-        y_step(t)
-        return c
-
-    lax.fori_loop(4, nz - 1, tail, 0)
-    finish(in_swap, fin_i, half, gin, 0)
-    y_step(nz - 1, last=True)
+    finish(out_swap, fin_o, zc, gout)
+    y_last()
+    finish(in_swap, fin_i, half, gin)
 
     for which, src, dst in ((0, stok, taken), (1, eout, rout), (2, gtak, rgrad)):
         sent_all(which, src, dst)
 
-    def grads_gone(i, c):
-        def body(k, c):
+    for i in range(len(chunks)):
+        def grads_gone(k, c, i=i):
             grad_chunk(i, (me + k) % n_ex, me).wait_send()
             return c
 
-        lax.fori_loop(1, n_ex, body, 0)
-        return c
-
-    lax.fori_loop(0, nz // 2, grads_gone, 0)
-
-    def ring_sent(t, c):
-        for d in (0, 1):
-            for j in (0, 1):
-                for which in (out_set, in_set, y_set):
-                    hop(*which, d, j, t).wait_send()
-        return c
-
-    lax.fori_loop(0, nz - 1, ring_sent, 0)
-
-    def across_sent(t, c):
-        for d in (0, 1):
-            across_copy(d, t).wait_send()
+        lax.fori_loop(1, n_ex, grads_gone, 0)
+
+    for flow in (out_flow, in_flow, y_flow):
+        for c in range(len(chains)):
+            for j in range(flow[0].shape[1]):
+                for t in range(hops - chains[c][2]):
+                    hop(flow, c, j, t).wait_send()
+
+    def across_sent(q, c):
+        across_copy(q).wait_send()
         return c
 
     lax.fori_loop(0, nz, across_sent, 0)
@@ -491,6 +479,7 @@
     half = hidden // 2
     zc = half * ZC // 8
     yc = half - zc
+    hops = nz // 2
     vmem = pl.BlockSpec(memory_space=pltpu.VMEM)
     hbm = pl.BlockSpec(memory_space=pl.ANY)
     dma = pltpu.SemaphoreType.DMA
@@ -522,36 +511,36 @@
             pltpu.VMEM((rows, width), BF),
             pltpu.VMEM((rows, width), BF),
             pltpu.VMEM((width, rows), BF),
-            pltpu.VMEM((2, blk, half), F32),
-            pltpu.VMEM((2, 2, nz, blk, zc // 2), BF),
-            pltpu.VMEM((2, 2, nz, blk, half // 2), BF),
-            pltpu.VMEM((2, 2, nz, blk // 2, yc // 2), BF),
-            pltpu.VMEM((2, nz, blk // 2, yc), F32),
-            pltpu.VMEM((2, nz, blk // 2, yc), BF),
-            pltpu.VMEM((2, nz, blk // 2, yc), BF),
-            pltpu.VMEM((2, 2, blk // 2, zc // 2), F32),
-            pltpu.VMEM((2, 2, blk // 2, half // 2), F32),
-            pltpu.VMEM((2, 2, blk // 2, zc // 2), BF),
-            pltpu.VMEM((2, 2, blk // 2, zc // 2), BF),
-            pltpu.VMEM((2, 2, blk // 2, half // 2), BF),
-            pltpu.VMEM((2, 2, blk // 2, half // 2), BF),
+            pltpu.VMEM((4, blk, half), F32),
+            pltpu.VMEM((4, SUBS[0], hops + 1, blk, zc // SUBS[0]), BF),
+            pltpu.VMEM((4, SUBS[1], hops + 1, blk, half // SUBS[1]), BF),
+            pltpu.VMEM((4, SUBS[2], hops + 1, blk // 2, yc // SUBS[2]), BF),
+            pltpu.VMEM((nz, blk // 2, 2 * yc), F32),
+            pltpu.VMEM((nz, blk // 2, 2 * yc), BF),
+            pltpu.VMEM((nz, blk // 2, 2 * yc), BF),
+            pltpu.VMEM((2, SUBS[0], blk // 2, zc // SUBS[0]), F32),
+            pltpu.VMEM((2, SUBS[1], blk // 2, half // SUBS[1]), F32),
+            pltpu.VMEM((2, SUBS[0], blk // 2, zc // SUBS[0]), BF),
+            pltpu.VMEM((2, SUBS[0], blk // 2, zc // SUBS[0]), BF),
+            pltpu.VMEM((2, SUBS[1], blk // 2, half // SUBS[1]), BF),
+            pltpu.VMEM((2, SUBS[1], blk // 2, half // SUBS[1]), BF),
             dma((4,)),
             dma((3, n_ex)),
             dma((3, n_ex)),
-            dma((nz // 2, n_ex)),
-            dma((nz // 2, n_ex)),
-            dma((2, 2, nz)),
-            dma((2, 2, nz)),
-            dma((2, 2, nz)),
-            dma((2, 2, nz)),
-            dma((2, 2, nz)),
-            dma((2, 2, nz)),
-            dma((2, nz)),
-            dma((2, nz)),
-            dma((2, 2)),
-            dma((2, 2)),
-            dma((2, 2)),
-            dma((2, 2)),
+            dma((4, n_ex)),
+            dma((4, n_ex)),
+            dma((4, SUBS[0], hops + 1)),
+            dma((4, SUBS[0], hops + 1)),
+            dma((4, SUBS[1], hops + 1)),
+            dma((4, SUBS[1], hops + 1)),
+            dma((4, SUBS[2], hops + 1)),
+            dma((4, SUBS[2], hops + 1)),
+            dma((nz,)),
+            dma((nz,)),
+            dma((2, SUBS[0])),
+            dma((2, SUBS[0])),
+            dma((2, SUBS[1])),
+            dma((2, SUBS[1])),
         ],
         compiler_params=pltpu.CompilerParams(
             collective_id=0, has_side_effects=True, vmem_limit_bytes=58 * 1024 * 1024

time: 120 us -> 112 us (0.933)
  Pallas kernels: 119 us -> 111 us
    pallas_call x1, Pallas kernels: 116 us -> 109 us  [on_device(): pl.pallas_call(functools.partial(kernel, n_dp, n_ex, zc), out_shape=(jax....]
where the time goes in v3:
time: 112 us
  Pallas kernels  111 us (99%)
    pallas_call x1, Pallas kernels, on_device(): pl.pallas_call(functools.partial(kernel, n_dp, n_ex, zc), out_shape=(jax....  109 us
    pallas_call x1, Pallas kernels, on_device(): pl.pallas_call(deliver, out_shape=tuple((jax.ShapeDtypeStruct(a.shape, a....  2.51 us

profile of v3, /device:TPU:4, one launch (start us, length us, event | category | flops | bytes accessed | tf_op | source)
XLA Modules:
  0.0 112.0 jit_solution(7783705955442967357)
XLA Ops:
  0.6 108.6 %shard_map.93 = (bf16[256,1024]{1,0:T(8,128)(2,1)}, bf16[256,1024]{1,0:T(8,128)(2,1)}, bf16[64,2048]{1,0:T(8,128)(2,1)}, bf16[64,2048]{1,0:T(8,128)(2,1)}) custom-call(bf16[256,1024]{1,0:T(8,128)(2,1)} %tok_hbm.1, s32[1,16,32]{2,1,0:T(8,128)} %pick.1, f32[1,16,32]{2,1,0:T(8,128)} %gate.1, bf16[1,1024,2048]{2,1,0:T(8,128)(2,1)} %win_hbm.1, ...), custom_call_target="tpu_custom_call" | custom-call | flops 12884901888 | bytes 10485760 | tf_op jit(solution)/shard_map/pallas_call | solution.py:486
  109.3 2.5 %shard_map.94 = (bf16[256,1024]{1,0:T(8,128)(2,1)}, bf16[256,1024]{1,0:T(8,128)(2,1)}, bf16[64,2048]{1,0:T(8,128)(2,1)}, bf16[64,2048]{1,0:T(8,128)(2,1)}) custom-call(bf16[256,1024]{1,0:T(8,128)(2,1)} %get-tuple-element.12.refs_0_, bf16[256,1024]{1,0:T(8,128)(2,1)} %get-tuple-element.13.refs_1_, bf16[64,2048]{1,0:T(8,128)(2,1)} %get-tuple-element.14.refs_2_, ...), custom_call_target="tpu_custom_call" | custom-call | tf_op jit(solution)/shard_map/pallas_call | solution.py:554

commit v4 on v3

--- a/solution.py
+++ b/solution.py
@@ -105,12 +105,24 @@
 
     pl.semaphore_wait(barrier, n_ex + 2)
 
-    def exchange(which, src, dst, peer, slot):
+    def landed(ref, sem):
+        pltpu.make_async_remote_copy(
+            src_ref=ref, dst_ref=ref, send_sem=sem, recv_sem=sem,
+            device_id={"dp": across}, device_id_type=MESH,
+        ).wait_recv()
+
+    def gone(ref, sem):
+        pltpu.make_async_remote_copy(
+            src_ref=ref, dst_ref=ref, send_sem=sem, recv_sem=sem,
+            device_id={"dp": across}, device_id_type=MESH,
+        ).wait_send()
+
+    def exchange(which, src, dst, peer):
         return pltpu.make_async_remote_copy(
             src_ref=src.at[pl.ds(peer * per, per)],
-            dst_ref=dst.at[pl.ds(slot * per, per)],
-            send_sem=tsend.at[which, peer],
-            recv_sem=trecv.at[which, slot],
+            dst_ref=dst.at[pl.ds(me * per, per)],
+            send_sem=tsend.at[which],
+            recv_sem=trecv.at[which],
             device_id={"expert": peer},
             device_id_type=MESH,
         )
@@ -118,61 +130,46 @@
     def peer_of(i):
         return (me + n_ex // 2 + (1 + i // 2) * (1 - 2 * (i % 2)) + n_ex) % n_ex
 
+    others = pl.ds(0, rows - per)
+
     def send_all(which, src, dst):
-        exchange(which, src, dst, (me + n_ex // 2) % n_ex, me).start()
+        exchange(which, src, dst, (me + n_ex // 2) % n_ex).start()
 
         def body(i, c):
-            exchange(which, src, dst, peer_of(i), me).start()
+            exchange(which, src, dst, peer_of(i)).start()
             return c
 
         lax.fori_loop(0, n_ex - 2, body, 0)
         own = pl.ds(me * per, per)
         dst[own, :] = src[own, :]
 
-    def recv_all(which, src, dst):
-        def body(k, c):
-            peer = (me + k) % n_ex
-            exchange(which, src, dst, peer, peer).wait_recv()
-            return c
-
-        lax.fori_loop(1, n_ex, body, 0)
-
-    def sent_all(which, src, dst):
-        def body(k, c):
-            exchange(which, src, dst, (me + k) % n_ex, me).wait_send()
-            return c
-
-        lax.fori_loop(1, n_ex, body, 0)
+    def recv_all(which, dst):
+        landed(dst.at[others], trecv.at[which])
 
     chunks = ((0, 1), (1, 2), (3, 2), (5, 3))
 
-    def grad_chunk(i, peer, slot):
+    def grad_chunk(i, peer):
         at = pl.ds(*chunks[i])
         return pltpu.make_async_remote_copy(
             src_ref=sgrad.at[at, pl.ds(peer * per, per)],
-            dst_ref=gsent.at[at, pl.ds(slot * per, per)],
-            send_sem=gsend.at[i, peer],
-            recv_sem=grecv.at[i, slot],
+            dst_ref=gsent.at[at, pl.ds(me * per, per)],
+            send_sem=gsend.at[0],
+            recv_sem=grecv.at[i],
             device_id={"expert": peer},
             device_id_type=MESH,
         )
 
     def send_grads(i):
-        grad_chunk(i, (me + n_ex // 2) % n_ex, me).start()
+        grad_chunk(i, (me + n_ex // 2) % n_ex).start()
 
         def body(k, c):
-            grad_chunk(i, peer_of(k), me).start()
+            grad_chunk(i, peer_of(k)).start()
             return c
 
         lax.fori_loop(0, n_ex - 2, body, 0)
 
     def recv_grads(i):
-        def body(k, c):
-            peer = (me + k) % n_ex
-            grad_chunk(i, peer, peer).wait_recv()
-            return c
-
-        lax.fori_loop(1, n_ex, body, 0)
+        landed(gsent.at[pl.ds(*chunks[i]), others], grecv.at[i])
 
     send_all(0, stok, taken)
     gate_col = column(dot(expert_of, g1) + dot(expert_of, g2) + dot(expert_of, g3))
@@ -231,22 +228,14 @@
         return pltpu.make_async_remote_copy(
             src_ref=ring.at[c, j, t],
             dst_ref=ring.at[c, j, t + 1],
-            send_sem=ssem.at[c, j, t],
-            recv_sem=rsem.at[c, j, t + 1],
-            device_id={"dp": (up, down)[chains[c][1]]},
-            device_id_type=MESH,
-        )
-
-    def arrived(flow, c, j, t):
-        ring, ssem, rsem = flow
-        pltpu.make_async_remote_copy(
-            src_ref=ring.at[c, j, t],
-            dst_ref=ring.at[c, j, t],
-            send_sem=ssem.at[c, j, t - 1],
+            send_sem=ssem.at[c],
             recv_sem=rsem.at[c, j, t],
             device_id={"dp": (up, down)[chains[c][1]]},
             device_id_type=MESH,
-        ).wait_recv()
+        )
+
+    def arrived(flow, c, j, t):
+        landed(flow[0].at[c, j, t], flow[2].at[c, j, t - 1])
 
     out_flow = (ring_o, osend, orecv)
     in_flow = (ring_i, isend, irecv)
@@ -260,31 +249,30 @@
         left = xt[pl.ds(pl.multiple_of(b * blk, blk), blk), :]
         return dot(left, gpre[:, c0 : c0 + n])
 
-    def pass_on(flow, c, t, values, w):
+    def pass_on(flow, c, j, t, value):
         ring = flow[0]
-        subs = ring.shape[1]
-        v = w // subs
-        for j in range(subs):
-            value = values(slice(j * v, (j + 1) * v))
-            if t > 0:
-                arrived(flow, c, j, t)
-                value = value + ring[c, j, t].astype(F32)
-            ring[c, j, t] = value.astype(BF)
-            hop(flow, c, j, t).start()
-
-    def z_step(flow, product, w, t, which):
+        if t > 0:
+            arrived(flow, c, j, t)
+            value = value + ring[c, j, t].astype(F32)
+        ring[c, j, t] = value.astype(BF)
+        hop(flow, c, j, t).start()
+
+    def z_step(flow, product, w, t, which, subs):
+        v = w // flow[0].shape[1]
         which = [c for c in which if t < hops - chains[c][2]]
         for c in which:
             h, d, p = chains[c]
-            part[c, :, :w] = product(place_of(d, t + p), h * w, w)
-        for c in which:
-            pass_on(flow, c, t, lambda cols, c=c: part[c, :, cols], w)
-
-    def out_step(t, which=(0, 1, 2, 3)):
-        z_step(out_flow, out_part, zc, t, which)
-
-    def in_step(t, which=(0, 1, 2, 3)):
-        z_step(in_flow, in_part, half, t, which)
+            c0, n = subs[0] * v, len(subs) * v
+            part[c, :, c0 : c0 + n] = product(place_of(d, t + p), h * w + c0, n)
+        for j in subs:
+            for c in which:
+                pass_on(flow, c, j, t, part[c, :, j * v : (j + 1) * v])
+
+    def out_step(t, which=(0, 1, 2, 3), subs=tuple(range(SUBS[0]))):
+        z_step(out_flow, out_part, half, t, which, subs)
+
+    def in_step(t, which=(0, 1, 2, 3), subs=tuple(range(SUBS[1]))):
+        z_step(in_flow, in_part, zc, t, which, subs)
 
     keep = pl.multiple_of(yh * half_rows, half_rows)
     give = pl.multiple_of((1 - yh) * half_rows, half_rows)
@@ -294,7 +282,7 @@
         return pltpu.make_async_remote_copy(
             src_ref=sbuf.at[h, j],
             dst_ref=rbuf.at[h, j],
-            send_sem=ssem.at[h, j],
+            send_sem=ssem.at[0],
             recv_sem=rsem.at[h, j],
             device_id={"dp": across},
             device_id_type=MESH,
@@ -328,7 +316,7 @@
         v = w // subs
         for h in (0, 1):
             for j in range(subs):
-                swap(swapping, h, j).wait()
+                swap(swapping, h, j).wait_recv()
                 c0 = h * w + j * v
                 out[:, c0 : c0 + v] = (fin[h, j] + swapping[1][h, j].astype(F32)).astype(BF)
 
@@ -336,7 +324,7 @@
         return pltpu.make_async_remote_copy(
             src_ref=ysend.at[q],
             dst_ref=yrecv.at[q],
-            send_sem=xsend.at[q],
+            send_sem=xsend.at[0],
             recv_sem=xrecv.at[q],
             device_id={"dp": across},
             device_id_type=MESH,
@@ -345,7 +333,7 @@
     def y_part(q):
         for h in (0, 1):
             cols = slice(h * yc, (h + 1) * yc)
-            part[h, :, :yc] = out_part(q, 2 * zc + h * yc, yc)
+            part[h, :, :yc] = in_part(q, 2 * zc + h * yc, yc)
             ysend[q, :, cols] = part[h, pl.ds(give, half_rows), :yc].astype(BF)
             ykeep[q, :, cols] = part[h, pl.ds(keep, half_rows), :yc]
         across_copy(q).start()
@@ -361,7 +349,9 @@
                 q = place_of(d, t + p)
                 if c >= 2 or q == 0 and c == 0:
                     across_copy(q).wait_recv()
-                pass_on(y_flow, c, t, lambda cols, q=q, h=h: y_sum(q, h, cols), yc)
+                v = yc // ring_y.shape[1]
+                for j in range(ring_y.shape[1]):
+                    pass_on(y_flow, c, j, t, y_sum(q, h, slice(j * v, (j + 1) * v)))
 
     def y_last():
         across_copy(nz - 1).wait_recv()
@@ -371,90 +361,80 @@
             for j in range(subs):
                 value = y_sum(nz - 1, h, slice(j * v, (j + 1) * v)) + both_arrived(y_flow, h, j)
                 c0 = 2 * zc + h * yc + j * v
-                gout[:, c0 : c0 + v] = value.astype(BF)
-
+                gin[:, c0 : c0 + v] = value.astype(BF)
+
+    all_tiles = hidden // tile
+    half_tiles = all_tiles // 2
+    sub_tiles = half_tiles // SUBS[0]
     loads[2].wait()
-    recv_all(0, stok, taken)
-    first_tiles = 2 * zc // tile
-    all_tiles = hidden // tile
-    lax.fori_loop(0, first_tiles, forward, 0)
-    recv_grads(0)
-    out_step(0, (0, 1))
-    middle_tile = (first_tiles + all_tiles) // 2
-    lax.fori_loop(first_tiles, middle_tile, forward, 0)
+    recv_all(0, taken)
+    for j in range(SUBS[0]):
+        for h in (0, 1):
+            t0 = h * half_tiles + j * sub_tiles
+            lax.fori_loop(t0, t0 + sub_tiles, forward, 0)
+        if j == 0:
+            recv_grads(0)
+        out_step(0, (0, 1), (j,))
     recv_grads(1)
     out_step(0, (2, 3))
-    lax.fori_loop(middle_tile, all_tiles, forward, 0)
-    for q in (0, 1, 2):
-        y_part(q)
-    out_step(1, (0, 1))
-    recv_grads(2)
-    out_step(1, (2, 3))
-    for q in (3, 4):
-        y_part(q)
+    xt[...] = taken[...].T
     loads[3].wait()
-    xt[...] = taken[...].T
     out_tiles = width // wtile
     lax.fori_loop(0, out_tiles, out_proj, 0)
+    recv_grads(2)
+    out_step(1, (0, 1), (0,))
     recv_grads(3)
     for q in range(nz):
         gflat[:, lane_block(block_at(q))] = gsent[q]
-    out_step(2)
-    lax.fori_loop(0, all_tiles // 2, backward, 0)
-    in_step(0, (0, 2))
-    lax.fori_loop(all_tiles // 2, all_tiles, backward, 0)
-    in_step(0, (1, 3))
-    for q in (5, 6, 7):
+    z_tiles = 2 * zc // tile
+    lax.fori_loop(z_tiles, all_tiles, backward, 0)
+    for j in range(1, SUBS[0]):
+        out_step(1, (0, 1), (j,))
+    for q in range(nz // 2):
         y_part(q)
-    out_step(3)
+    out_step(1, (2, 3))
+    for q in range(nz // 2, nz):
+        y_part(q)
+    lax.fori_loop(0, z_tiles, backward, 0)
+    in_step(0)
     send_all(1, eout, rout)
     lax.fori_loop(0, out_tiles, grad_tokens, 0)
     send_all(2, gtak, rgrad)
+    out_step(2)
     in_step(1)
     y_step(0)
-    last_step(out_flow, out_part, out_swap, fin_o, zc)
+    out_step(3)
     in_step(2)
     y_step(1)
     in_step(3)
-
-    recv_all(1, eout, rout)
+    last_step(out_flow, out_part, out_swap, fin_o, half)
+
+    recv_all(1, rout)
     selt = lax.broadcasted_iota(jnp.int32, (tokens, rows), 0).astype(F32) == pick_row
     hi = gate_row.astype(BF).astype(F32)
     mixed[...] = (
         dot(jnp.where(selt, hi, 0.0).astype(BF), rout[...])
         + dot(jnp.where(selt, gate_row - hi, 0.0).astype(BF), rout[...])
     ).astype(BF)
-    recv_all(2, gtak, rgrad)
+    recv_all(2, rgrad)
     tgrad[...] = dot(selt.astype(F32).astype(BF), rgrad[...]).astype(BF)
 
     y_step(2)
-    last_step(in_flow, in_part, in_swap, fin_i, half)
+    last_step(in_flow, in_part, in_swap, fin_i, zc)
     y_step(3)
-    finish(out_swap, fin_o, zc, gout)
+    finish(out_swap, fin_o, half, gout)
     y_last()
-    finish(in_swap, fin_i, half, gin)
-
-    for which, src, dst in ((0, stok, taken), (1, eout, rout), (2, gtak, rgrad)):
-        sent_all(which, src, dst)
-
-    for i in range(len(chunks)):
-        def grads_gone(k, c, i=i):
-            grad_chunk(i, (me + k) % n_ex, me).wait_send()
-            return c
-
-        lax.fori_loop(1, n_ex, grads_gone, 0)
-
-    for flow in (out_flow, in_flow, y_flow):
+    finish(in_swap, fin_i, zc, gin)
+
+    for which, src in enumerate((stok, eout, gtak)):
+        gone(src.at[others], tsend.at[which])
+    gone(sgrad.at[:, others], gsend.at[0])
+    for ring, ssem, _ in (out_flow, in_flow, y_flow):
         for c in range(len(chains)):
-            for j in range(flow[0].shape[1]):
-                for t in range(hops - chains[c][2]):
-                    hop(flow, c, j, t).wait_send()
-
-    def across_sent(q, c):
-        across_copy(q).wait_send()
-        return c
-
-    lax.fori_loop(0, nz, across_sent, 0)
+            gone(ring.at[c, :, pl.ds(0, hops - chains[c][2])], ssem.at[c])
+    gone(swap_so, sosend.at[0])
+    gone(swap_si, sisend.at[0])
+    gone(ysend, xsend.at[0])
 
 
 def deliver(*refs):
@@ -512,34 +492,34 @@
             pltpu.VMEM((rows, width), BF),
             pltpu.VMEM((width, rows), BF),
             pltpu.VMEM((4, blk, half), F32),
-            pltpu.VMEM((4, SUBS[0], hops + 1, blk, zc // SUBS[0]), BF),
-            pltpu.VMEM((4, SUBS[1], hops + 1, blk, half // SUBS[1]), BF),
+            pltpu.VMEM((4, SUBS[0], hops + 1, blk, half // SUBS[0]), BF),
+            pltpu.VMEM((4, SUBS[1], hops + 1, blk, zc // SUBS[1]), BF),
             pltpu.VMEM((4, SUBS[2], hops + 1, blk // 2, yc // SUBS[2]), BF),
             pltpu.VMEM((nz, blk // 2, 2 * yc), F32),
             pltpu.VMEM((nz, blk // 2, 2 * yc), BF),
             pltpu.VMEM((nz, blk // 2, 2 * yc), BF),
-            pltpu.VMEM((2, SUBS[0], blk // 2, zc // SUBS[0]), F32),
-            pltpu.VMEM((2, SUBS[1], blk // 2, half // SUBS[1]), F32),
-            pltpu.VMEM((2, SUBS[0], blk // 2, zc // SUBS[0]), BF),
-            pltpu.VMEM((2, SUBS[0], blk // 2, zc // SUBS[0]), BF),
-            pltpu.VMEM((2, SUBS[1], blk // 2, half // SUBS[1]), BF),
-            pltpu.VMEM((2, SUBS[1], blk // 2, half // SUBS[1]), BF),
+            pltpu.VMEM((2, SUBS[0], blk // 2, half // SUBS[0]), F32),
+            pltpu.VMEM((2, SUBS[1], blk // 2, zc // SUBS[1]), F32),
+            pltpu.VMEM((2, SUBS[0], blk // 2, half // SUBS[0]), BF),
+            pltpu.VMEM((2, SUBS[0], blk // 2, half // SUBS[0]), BF),
+            pltpu.VMEM((2, SUBS[1], blk // 2, zc // SUBS[1]), BF),
+            pltpu.VMEM((2, SUBS[1], blk // 2, zc // SUBS[1]), BF),
             dma((4,)),
-            dma((3, n_ex)),
-            dma((3, n_ex)),
-            dma((4, n_ex)),
-            dma((4, n_ex)),
-            dma((4, SUBS[0], hops + 1)),
-            dma((4, SUBS[0], hops + 1)),
-            dma((4, SUBS[1], hops + 1)),
-            dma((4, SUBS[1], hops + 1)),
-            dma((4, SUBS[2], hops + 1)),
-            dma((4, SUBS[2], hops + 1)),
+            dma((3,)),
+            dma((3,)),
+            dma((1,)),
+            dma((4,)),
+            dma((4,)),
+            dma((4, SUBS[0], hops)),
+            dma((4,)),
+            dma((4, SUBS[1], hops)),
+            dma((4,)),
+            dma((4, SUBS[2], hops)),
+            dma((1,)),
             dma((nz,)),
-            dma((nz,)),
+            dma((1,)),
             dma((2, SUBS[0])),
-            dma((2, SUBS[0])),
-            dma((2, SUBS[1])),
+            dma((1,)),
             dma((2, SUBS[1])),
         ],
         compiler_params=pltpu.CompilerParams(

time: 112 us -> 105 us (0.938)
  Pallas kernels: 111 us -> 103 us
    pallas_call x1, Pallas kernels: 109 us -> 101 us  [on_device(): pl.pallas_call(functools.partial(kernel, n_dp, n_ex, zc), out_shape=(jax....]
where the time goes in v4:
time: 105 us; the launch traced here: 104 us
  Pallas kernels  103 us (98%)
    pallas_call x1, Pallas kernels, on_device(): pl.pallas_call(functools.partial(kernel, n_dp, n_ex, zc), out_shape=(jax....  101 us
    pallas_call x1, Pallas kernels, on_device(): pl.pallas_call(deliver, out_shape=tuple((jax.ShapeDtypeStruct(a.shape, a....  2.51 us

profile of v4, /device:TPU:4, one launch (start us, length us, event | category | flops | bytes accessed | tf_op | source)
XLA Modules:
  0.0 104.0 jit_solution(6335221359000031970)
XLA Ops:
  0.6 100.7 %shard_map.93 = (bf16[256,1024]{1,0:T(8,128)(2,1)}, bf16[256,1024]{1,0:T(8,128)(2,1)}, bf16[64,2048]{1,0:T(8,128)(2,1)}, bf16[64,2048]{1,0:T(8,128)(2,1)}) custom-call(bf16[256,1024]{1,0:T(8,128)(2,1)} %tok_hbm.1, s32[1,16,32]{2,1,0:T(8,128)} %pick.1, f32[1,16,32]{2,1,0:T(8,128)} %gate.1, bf16[1,1024,2048]{2,1,0:T(8,128)(2,1)} %win_hbm.1, ...), custom_call_target="tpu_custom_call" | custom-call | flops 12884901888 | bytes 10485760 | tf_op jit(solution)/shard_map/pallas_call | solution.py:466
  101.3 2.5 %shard_map.94 = (bf16[256,1024]{1,0:T(8,128)(2,1)}, bf16[256,1024]{1,0:T(8,128)(2,1)}, bf16[64,2048]{1,0:T(8,128)(2,1)}, bf16[64,2048]{1,0:T(8,128)(2,1)}) custom-call(bf16[256,1024]{1,0:T(8,128)(2,1)} %get-tuple-element.12.refs_0_, bf16[256,1024]{1,0:T(8,128)(2,1)} %get-tuple-element.13.refs_1_, bf16[64,2048]{1,0:T(8,128)(2,1)} %get-tuple-element.14.refs_2_, ...), custom_call_target="tpu_custom_call" | custom-call | tf_op jit(solution)/shard_map/pallas_call | solution.py:534

commit v5 on v4

--- a/solution.py
+++ b/solution.py
@@ -11,8 +11,8 @@
 BF = jnp.bfloat16
 F32 = jnp.float32
 NT = (((1,), (1,)), ((), ()))
-ZC = 4
-SUBS = (2, 2, 1)
+ZC = 3
+SUBS = (4, 3, 1)
 
 
 def dot(a, b):
@@ -26,11 +26,11 @@
 def kernel(
     n_dp, n_ex, zc,
     tok_hbm, pick, gate, win_hbm, wout_hbm, cot_hbm,
-    mixed, tgrad, gin, gout,
-    win, wout, tok, cot, stok, sgrad, taken, gsent, gflat, act, dgel, gpre, eout, gtak, rout, rgrad,
+    mixed_hbm, tgrad_hbm, gin_hbm, gout_hbm,
+    mixed, tgrad, gin, gout, win, wout, tok, cot, stok, sgrad, taken, gsent, gflat, act, dgel, gpre, eout, gtak, rout, rgrad,
     xt, part, ring_o, ring_i, ring_y, ykeep, ysend, yrecv,
     fin_o, fin_i, swap_so, swap_ro, swap_si, swap_ri,
-    wsem, tsend, trecv, gsend, grecv,
+    wsem, ressem, tsend, trecv, gsend, grecv,
     osend, orecv, isend, irecv, rysend, ryrecv, xsend, xrecv,
     sosend, sorecv, sisend, sirecv,
 ):
@@ -51,6 +51,18 @@
     down = (r + n_dp - 2) % n_dp
     across = r + 1 - 2 * yh
 
+    barrier = pltpu.get_barrier_semaphore()
+
+    def greet(k, c):
+        pl.semaphore_signal(
+            barrier, inc=1, device_id={"expert": (me + k) % n_ex}, device_id_type=MESH
+        )
+        return c
+
+    lax.fori_loop(1, n_ex, greet, 0)
+    for other in (up, down, across):
+        pl.semaphore_signal(barrier, inc=1, device_id={"dp": other}, device_id_type=MESH)
+
     loads = [
         pltpu.make_async_copy(src, dst, wsem.at[i])
         for i, (src, dst) in enumerate(
@@ -59,27 +71,15 @@
     ]
     for load in loads:
         load.start()
-
-    barrier = pltpu.get_barrier_semaphore()
-
-    def greet(k, c):
-        pl.semaphore_signal(
-            barrier, inc=1, device_id={"expert": (me + k) % n_ex}, device_id_type=MESH
-        )
-        return c
-
-    lax.fori_loop(1, n_ex, greet, 0)
-    for other in (up, down, across):
-        pl.semaphore_signal(barrier, inc=1, device_id={"dp": other}, device_id_type=MESH)
 
     p2 = pick[0].astype(F32).astype(BF)
     g = gate[0]
     g1 = g.astype(BF)
     g2 = (g - g1.astype(F32)).astype(BF)
     g3 = (g - g1.astype(F32) - g2.astype(F32)).astype(BF)
-    row_e = lax.broadcasted_iota(jnp.int32, (rows, n_ex), 0) // per
+    row_e = lax.broadcasted_iota(jnp.int32, (n_ex, per, n_ex), 0).reshape(rows, n_ex)
     expert_of = (row_e == lax.broadcasted_iota(jnp.int32, (rows, n_ex), 1)).astype(F32).astype(BF)
-    place = lax.broadcasted_iota(jnp.int32, (rows, per), 0) % per
+    place = lax.broadcasted_iota(jnp.int32, (n_ex, per, per), 1).reshape(rows, per)
     here = place == lax.broadcasted_iota(jnp.int32, (rows, per), 1)
 
     def column(values):
@@ -183,9 +183,9 @@
         gsent[q, mine, :] = sgrad[q, mine, :]
 
     here_bf = here.astype(F32).astype(BF)
-    own_e = lax.broadcasted_iota(jnp.int32, (n_ex, rows), 0) == (
-        lax.broadcasted_iota(jnp.int32, (n_ex, rows), 1) // per
-    )
+    first = per * lax.broadcasted_iota(jnp.int32, (n_ex, rows), 0)
+    at_row = lax.broadcasted_iota(jnp.int32, (n_ex, rows), 1)
+    own_e = (at_row >= first) & (at_row < first + per)
 
     def as_row(values):
         return jnp.sum(jnp.where(own_e, values, 0.0), axis=0, keepdims=True)
@@ -384,6 +384,7 @@
     recv_grads(2)
     out_step(1, (0, 1), (0,))
     recv_grads(3)
+    send_all(1, eout, rout)
     for q in range(nz):
         gflat[:, lane_block(block_at(q))] = gsent[q]
     z_tiles = 2 * zc // tile
@@ -397,7 +398,6 @@
         y_part(q)
     lax.fori_loop(0, z_tiles, backward, 0)
     in_step(0)
-    send_all(1, eout, rout)
     lax.fori_loop(0, out_tiles, grad_tokens, 0)
     send_all(2, gtak, rgrad)
     out_step(2)
@@ -409,6 +409,9 @@
     in_step(3)
     last_step(out_flow, out_part, out_swap, fin_o, half)
 
+    def store(i, src, dst):
+        return pltpu.make_async_copy(src, dst, ressem.at[i])
+
     recv_all(1, rout)
     selt = lax.broadcasted_iota(jnp.int32, (tokens, rows), 0).astype(F32) == pick_row
     hi = gate_row.astype(BF).astype(F32)
@@ -416,15 +419,19 @@
         dot(jnp.where(selt, hi, 0.0).astype(BF), rout[...])
         + dot(jnp.where(selt, gate_row - hi, 0.0).astype(BF), rout[...])
     ).astype(BF)
+    store(0, mixed, mixed_hbm).start()
     recv_all(2, rgrad)
     tgrad[...] = dot(selt.astype(F32).astype(BF), rgrad[...]).astype(BF)
+    store(1, tgrad, tgrad_hbm).start()
 
     y_step(2)
     last_step(in_flow, in_part, in_swap, fin_i, zc)
     y_step(3)
     finish(out_swap, fin_o, half, gout)
+    store(2, gout, gout_hbm).start()
     y_last()
     finish(in_swap, fin_i, zc, gin)
+    store(3, gin, gin_hbm).start()
 
     for which, src in enumerate((stok, eout, gtak)):
         gone(src.at[others], tsend.at[which])
@@ -435,18 +442,25 @@
     gone(swap_so, sosend.at[0])
     gone(swap_si, sisend.at[0])
     gone(ysend, xsend.at[0])
+    store(0, mixed, mixed_hbm).wait()
+    store(1, tgrad, tgrad_hbm).wait()
+    store(2, gout, gout_hbm).wait()
+    store(3, gin, gin_hbm).wait()
 
 
 def deliver(*refs):
-    sem = refs[-1]
-    count = len(refs) // 2
-    copies = [
-        pltpu.make_async_copy(refs[i], refs[count + i], sem.at[i]) for i in range(count)
-    ]
-    for copy in copies:
-        copy.start()
-    for copy in copies:
-        copy.wait()
+    count = len(refs) // 3
+    source, target, held = (refs[i * count : (i + 1) * count] for i in range(3))
+    loaded, stored = refs[3 * count :]
+    loads = [pltpu.make_async_copy(source[i], held[i], loaded.at[i]) for i in range(count)]
+    stores = [pltpu.make_async_copy(held[i], target[i], stored.at[i]) for i in range(count)]
+    for load in loads:
+        load.start()
+    for load, store in zip(loads, stores):
+        load.wait()
+        store.start()
+    for store in stores:
+        store.wait()
 
 
 def on_device(n_dp, n_ex, tokens, picks, gates, w_in, w_out, cotangent):
@@ -472,8 +486,12 @@
             jax.ShapeDtypeStruct((width // n_dp, hidden), BF),
         ),
         in_specs=[hbm, vmem, vmem, hbm, hbm, hbm],
-        out_specs=(vmem, vmem, vmem, vmem),
+        out_specs=(hbm, hbm, hbm, hbm),
         scratch_shapes=[
+            pltpu.VMEM((count, width), BF),
+            pltpu.VMEM((count, width), BF),
+            pltpu.VMEM((width // n_dp, hidden), BF),
+            pltpu.VMEM((width // n_dp, hidden), BF),
             pltpu.VMEM((width, hidden), BF),
             pltpu.VMEM((hidden, width), BF),
             pltpu.VMEM((count, width), BF),
@@ -504,6 +522,7 @@
             pltpu.VMEM((2, SUBS[0], blk // 2, half // SUBS[0]), BF),
             pltpu.VMEM((2, SUBS[1], blk // 2, zc // SUBS[1]), BF),
             pltpu.VMEM((2, SUBS[1], blk // 2, zc // SUBS[1]), BF),
+            dma((4,)),
             dma((4,)),
             dma((3,)),
             dma((3,)),
@@ -534,9 +553,9 @@
     mixed, tgrad, gin, gout = pl.pallas_call(
         deliver,
         out_shape=tuple(jax.ShapeDtypeStruct(a.shape, a.dtype) for a in results),
-        in_specs=[vmem] * 4,
+        in_specs=[hbm] * 4,
         out_specs=(hbm,) * 4,
-        scratch_shapes=[dma((4,))],
+        scratch_shapes=[pltpu.VMEM(a.shape, a.dtype) for a in results] + [dma((4,)), dma((4,))],
         compiler_params=pltpu.CompilerParams(vmem_limit_bytes=58 * 1024 * 1024),
     )(*results)
     return mixed, tgrad, gin[:, None, :], gout[:, None, :]

time: 105 us -> 102 us (0.971)
  Pallas kernels: 103 us -> 99.6 us
    pallas_call x1, Pallas kernels: 101 us -> 97.3 us  [on_device(): pl.pallas_call(functools.partial(kernel, n_dp, n_ex, zc), out_shape=(jax....]
where the time goes in v5:
time: 102 us; the launch traced here: 100 us
  Pallas kernels  99.6 us (98%)
    pallas_call x1, Pallas kernels, on_device(): pl.pallas_call(functools.partial(kernel, n_dp, n_ex, zc), out_shape=(jax....  97.3 us
    pallas_call x1, Pallas kernels, on_device(): pl.pallas_call(deliver, out_shape=tuple((jax.ShapeDtypeStruct(a.shape, a....  2.25 us

profile of v5, /device:TPU:4, one launch (start us, length us, event | category | flops | bytes accessed | tf_op | source)
XLA Modules:
  0.0 100.4 jit_solution(3217303181567372639)
XLA Ops:
  0.6 97.3 %shard_map.93 = (bf16[256,1024]{1,0:T(8,128)(2,1)}, bf16[256,1024]{1,0:T(8,128)(2,1)}, bf16[64,2048]{1,0:T(8,128)(2,1)}, bf16[64,2048]{1,0:T(8,128)(2,1)}) custom-call(bf16[256,1024]{1,0:T(8,128)(2,1)} %tok_hbm.1, s32[1,16,32]{2,1,0:T(8,128)} %pick.1, f32[1,16,32]{2,1,0:T(8,128)} %gate.1, bf16[1,1024,2048]{2,1,0:T(8,128)(2,1)} %win_hbm.1, ...), custom_call_target="tpu_custom_call" | custom-call | flops 12884901888 | bytes 10485760 | tf_op jit(solution)/shard_map/pallas_call | solution.py:480
  98.0 2.2 %shard_map.94 = (bf16[256,1024]{1,0:T(8,128)(2,1)}, bf16[256,1024]{1,0:T(8,128)(2,1)}, bf16[64,2048]{1,0:T(8,128)(2,1)}, bf16[64,2048]{1,0:T(8,128)(2,1)}) custom-call(bf16[256,1024]{1,0:T(8,128)(2,1)} %get-tuple-element.12.refs_0_, bf16[256,1024]{1,0:T(8,128)(2,1)} %get-tuple-element.13.refs_1_, bf16[64,2048]{1,0:T(8,128)(2,1)} %get-tuple-element.14.refs_2_, ...), custom_call_target="tpu_custom_call" | custom-call | tf_op jit(solution)/shard_map/pallas_call | solution.py:553
